TPU v7x, 512 devices: a whole 4x8x8 slice. The times are simulated.
512 devices in a mesh: branch: 2 (over y_hi), trow: 8 (over z), tcol: 32 (over x, y_lo, core).
Axes of the slice: x: 4, y: 8 (y_hi: 2, y_lo: 4; y = y_hi * 4 + y_lo), z: 8, core: 2. Of those that a mesh axis runs over, the one named last changes fastest.
Arguments:
- latent: bfloat16 [2, 2, 64, 256, 1152], P('branch', None, 'trow', 'tcol'), may hold values from -6 to 6
- modulation: float32 [2, 3, 1152], replicated, may hold values from -2 to 2
- w_query: bfloat16 [2, 1152, 576], P('branch', None, 'tcol'), may hold values from -0.176776695 to 0.176776695
- w_keyval: bfloat16 [2, 1152, 1152], P('branch', None, 'tcol'), may hold values from -3.8301617 to 3.8301617
- w_out: bfloat16 [2, 576, 1152], P('branch', 'tcol'), may hold values from -0.25 to 0.25
- w_zero: bfloat16 [1152, 1152], P(None, 'tcol'), may hold values from -0.1875 to 0.1875
Outputs:
- hidden_out: bfloat16 [2, 2, 64, 256, 1152], P('branch', None, 'trow', 'tcol')
All inputs are finite; a program needn't handle non-finite values.
Results may differ from a plain program's by a relative error of at most 0.0075.
Values may be sent and summed in bfloat16 or wider, within the bound.
A program may use at most 128 MiB of HBM per device.

v0:
```python
import math

import jax
import jax.numpy as jnp
from jax import lax
from jax.sharding import PartitionSpec as P

D = 1152
HD = 72
HEADS = 8
WIN = 13
HW = 576


def padded(block, sides, width):
    for axis, dim in sides:
        count = lax.axis_size(axis)
        forward = [(i, i + 1) for i in range(count - 1)]
        backward = [(target, source) for source, target in forward]
        low = lax.ppermute(
            lax.slice_in_dim(block, block.shape[dim] - width, None, axis=dim), axis, forward
        )
        high = lax.ppermute(lax.slice_in_dim(block, 0, width, axis=dim), axis, backward)
        block = jnp.concatenate([low, block, high], axis=dim)
    return block


def shifted(block, axis, distance):
    devices = range(lax.axis_size(axis))
    route = [(i - distance, i) for i in devices if i - distance in devices]
    return lax.ppermute(block, axis, route)


def modulate(hidden, shift_scale):
    average = jnp.mean(hidden, axis=-1, keepdims=True)
    centred = hidden - average
    variance = jnp.mean(centred * centred, axis=-1, keepdims=True)
    return (centred * lax.rsqrt(variance + 1e-06) * (1.0 + shift_scale[1]) + shift_scale[0]).astype(
        jnp.bfloat16
    )


def block_mask(row_first, col_first, total_rows, total_cols, key_count):
    query_edge = 8
    radius = WIN // 2
    key_side = query_edge + 2 * radius
    offsets = jnp.arange(query_edge)
    reaches = jnp.arange(key_side)
    row_starts = jnp.clip(row_first + offsets - radius, 0, total_rows - WIN)
    key_rows = row_first - radius + reaches
    row_inside = (key_rows[None, :] >= row_starts[:, None]) & (
        key_rows[None, :] < row_starts[:, None] + WIN
    )
    col_starts = jnp.clip(col_first + offsets - radius, 0, total_cols - WIN)
    key_cols = col_first - radius + reaches
    col_inside = (key_cols[None, :] >= col_starts[:, None]) & (
        key_cols[None, :] < col_starts[:, None] + WIN
    )
    joined = row_inside[:, None, :, None] & col_inside[None, :, None, :]
    joined = joined.reshape(query_edge * query_edge, key_side * key_side)
    filler = jnp.zeros((query_edge * query_edge, key_count - key_side * key_side), dtype=jnp.bool_)
    return jnp.concatenate([joined, filler], axis=1)


def edge_keys(key_values):
    radius = WIN // 2
    return padded(key_values, (("trow", 1), ("tcol", 2)), radius)


def attend_tile(queries, extended, row_anchor, col_anchor, total_rows, total_cols):
    images, tile_rows, tile_cols = (queries.shape[0], queries.shape[1], queries.shape[2])
    query_edge = 8
    radius = WIN // 2
    key_side = query_edge + 2 * radius
    key_count = (key_side * key_side + 127) // 128 * 128
    across = tile_cols // query_edge
    block_count = tile_rows // query_edge * across
    scaling = 1.0 / math.sqrt(HD)

    def one_block(position):
        row_block = position // across * query_edge
        col_block = position % across * query_edge
        query_block = queries
        query_block = query_block.reshape(images, query_edge * query_edge, HEADS, HD)
        key_block = extended
        key_block = key_block.reshape(images, key_side * key_side, 2 * HW)
        key_block = jnp.pad(key_block, ((0, 0), (0, key_count - key_side * key_side), (0, 0)))
        key_heads = key_block[..., :HW].reshape(images, key_count, HEADS, HD)
        value_heads = key_block[..., HW:].reshape(images, key_count, HEADS, HD)
        allowed = block_mask(
            row_anchor + row_block, col_anchor + col_block, total_rows, total_cols, key_count
        )
        scores = (
            jnp.einsum(
                "iqhd,ikhd->ihqk", query_block, key_heads, preferred_element_type=jnp.float32
            )
            * scaling
        )
        scores = jnp.where(allowed[None, None], scores, -1e30)
        highest = jnp.max(scores, axis=-1, keepdims=True)
        raised = jnp.exp(scores - highest)
        totals = jnp.sum(raised, axis=-1, keepdims=True)
        weights = (raised / totals).astype(jnp.bfloat16)
        blended = jnp.einsum(
            "ihqk,ikhd->iqhd", weights, value_heads, preferred_element_type=jnp.float32
        )
        return blended.astype(jnp.bfloat16).reshape(images, query_edge, query_edge, HW)

    result = lax.map(one_block, jnp.arange(block_count))
    result = result.reshape(tile_rows // query_edge, across, images, query_edge, query_edge, HW)
    return result.transpose(2, 0, 3, 1, 4, 5).reshape(images, tile_rows, tile_cols, HW)


def run_block(active, hidden, shift_scale, weight_q, weight_kv, weight_o):
    images, tile_rows, tile_cols = (hidden.shape[0], hidden.shape[1], hidden.shape[2])
    tokens = images * tile_rows * tile_cols

    def project():
        flattened = modulate(hidden, shift_scale).reshape(tokens, D)
        queries = jnp.dot(flattened, weight_q, preferred_element_type=jnp.float32).astype(
            jnp.bfloat16
        )
        key_values = jnp.dot(flattened, weight_kv, preferred_element_type=jnp.float32).astype(
            jnp.bfloat16
        )
        return (queries, key_values)

    def nothing():
        return (jnp.zeros((tokens, HW), jnp.bfloat16), jnp.zeros((tokens, 2 * HW), jnp.bfloat16))

    queries, key_values = lax.cond(active, project, nothing)
    extended = edge_keys(key_values.reshape(images, tile_rows, tile_cols, 2 * HW))
    row_anchor = lax.axis_index("trow") * tile_rows
    col_anchor = lax.axis_index("tcol") * tile_cols
    total_rows = tile_rows * lax.axis_size("trow")
    total_cols = tile_cols * lax.axis_size("tcol")

    def finish():
        attended = attend_tile(
            queries.reshape(images, tile_rows, tile_cols, HW),
            extended,
            row_anchor,
            col_anchor,
            total_rows,
            total_cols,
        )
        projected = jnp.dot(
            attended.reshape(tokens, HW), weight_o, preferred_element_type=jnp.float32
        )
        return (hidden + shift_scale[2] * projected.reshape(hidden.shape)).astype(jnp.bfloat16)

    def vacant():
        return jnp.zeros(hidden.shape, jnp.bfloat16)

    return lax.cond(active, finish, vacant)


def zero_project(control_out, weight_z):
    flattened = control_out.reshape(-1, D)
    return (
        jnp.dot(flattened, weight_z, preferred_element_type=jnp.float32)
        .astype(jnp.bfloat16)
        .reshape(control_out.shape)
    )


def on_device(latent, modulation, w_query, w_keyval, w_out, w_zero):
    sources = (w_query, w_keyval, w_out)
    weight_q, weight_kv, weight_o, weight_z = (
        lax.all_gather(sources[0], "tcol", axis=2, tiled=True),
        lax.all_gather(sources[1], "tcol", axis=2, tiled=True),
        lax.all_gather(sources[2], "tcol", axis=1, tiled=True),
        lax.all_gather(w_zero, "tcol", axis=1, tiled=True),
    )
    branch_index = lax.axis_index("branch")
    is_control = branch_index == 1
    own_copy = latent[0]
    shift_scale = lax.dynamic_index_in_dim(modulation, branch_index, 0, keepdims=False)
    received = shifted(own_copy, "branch", 1)
    control_in = own_copy.astype(jnp.float32) + received.astype(jnp.float32)
    control_out = run_block(
        is_control, control_in, shift_scale, weight_q[0], weight_kv[0], weight_o[0]
    )

    def with_projection():
        return zero_project(control_out, weight_z)

    def without_projection():
        return jnp.zeros(control_out.shape, jnp.bfloat16)

    residual = lax.cond(is_control, with_projection, without_projection)
    returned = shifted(residual, "branch", -1)
    base_in = own_copy.astype(jnp.float32) + returned.astype(jnp.float32)
    base_out = run_block(
        jnp.logical_not(is_control), base_in, shift_scale, weight_q[0], weight_kv[0], weight_o[0]
    )
    return jnp.where(is_control, control_out, base_out)[None]


def solution(mesh):
    placed = (
        P("branch", None, "trow", "tcol", None),
        P(),
        P("branch", None, "tcol"),
        P("branch", None, "tcol"),
        P("branch", "tcol", None),
        P(None, "tcol"),
    )
    return jax.shard_map(
        on_device,
        mesh=mesh,
        in_specs=placed,
        out_specs=P("branch", None, "trow", "tcol", None),
        check_vma=False,
    )
```

profile of v0, /device:TPU:1, one launch (start us, length us, event | category | flops | bytes accessed | tf_op | source)
XLA Modules:
  0.0 417.9 jit_solution(13802482478232100090)
XLA Ops:
  12.0 8.3 %collective-permute-start = (bf16[2,8,8,1152]{3,2,1,0:T(8,128)(2,1)}, bf16[2,8,8,1152]{3,2,1,0:T(8,128)(2,1)S(1)}, u32[]{:S(2)}, u32[]{:S(2)}) collective-permute-start(bf16[2,8,8,1152]{3,2,1,0:T(8,128)(2,1)} %bitcast.100), channel_id=1, source_target_pairs={{0,256},{1,257},{2,258},{3,259},{4,260},{5,261},{6,262},{7,263},{8... | collective-permute-start | bytes 884744 | tf_op jit(solution)/shard_map/ppermute | solution.py:31
  20.4 5.9 %collective-permute-done = bf16[2,8,8,1152]{3,2,1,0:T(8,128)(2,1)S(1)} collective-permute-done((bf16[2,8,8,1152]{3,2,1,0:T(8,128)(2,1)}, bf16[2,8,8,1152]{3,2,1,0:T(8,128)(2,1)S(1)}, u32[]{:S(2)}, u32[]{:S(2)}) %collective-permute-start) | collective-permute-done | bytes 294944 | tf_op jit(solution)/shard_map/ppermute | solution.py:31
  27.3 51.8 %all-gather.6.cloned.1.call-done = bf16[1,1152,576]{1,0,2:T(2,128)(2,1)} async-done(((bf16[1,1152,18]{1,0,2:T(2,128)(2,1)}), bf16[1,1152,576]{1,0,2:T(2,128)(2,1)}) %all-gather.6.cloned.1.call-update) | async-done | bytes 1327120 | tf_op jit(solution)/shard_map/all_gather | solution.py:170
  82.1 68.8 %all-gather.8.cloned.1.call-done = bf16[1,1152,1152]{1,0,2:T(2,128)(2,1)} async-done(((bf16[1,1152,36]{1,0,2:T(2,128)(2,1)}), bf16[1,1152,1152]{1,0,2:T(2,128)(2,1)}) %all-gather.8.cloned.1.call-update) | async-done | bytes 2654224 | tf_op jit(solution)/shard_map/all_gather | solution.py:171
  150.9 10.9 %copy.67 = bf16[1,1152,1152]{2,1,0:T(8,128)(2,1)S(1)} copy(bf16[1,1152,1152]{1,0,2:T(2,128)(2,1)} %all-gather.8.cloned.1.call-done) | data formatting | bytes 5308416 | tf_op jit(solution)/shard_map/all_gather | solution.py:171
  165.0 4.0 collective-permute-start.1
  169.0 3.3 collective-permute-done.2
  176.4 3.3 collective-permute-start.4
  183.5 38.2 %all-gather.10.cloned.1.call-done = bf16[1,576,1152]{2,0,1:T(2,128)(2,1)} async-done(((bf16[1,18,1152]{2,0,1:T(2,128)(2,1)}), bf16[1,576,1152]{2,0,1:T(2,128)(2,1)}) %all-gather.10.cloned.1.call-update) | async-done | bytes 1327120 | tf_op jit(solution)/shard_map/all_gather | solution.py:172
  224.7 63.1 %all-gather.12.cloned.1.call-done = bf16[32,36,1152]{2,1,0:T(8,128)(2,1)} async-done(((bf16[1,36,1152]{2,1,0:T(8,128)(2,1)}), bf16[32,36,1152]{2,1,0:T(8,128)(2,1)}) %all-gather.12.cloned.1.call-update) | async-done | bytes 2654224 | tf_op jit(solution)/shard_map/all_gather | solution.py:173
  287.8 5.2 %reshape.395 = bf16[1152,1152]{1,0:T(8,128)(2,1)} reshape(bf16[32,36,1152]{2,1,0:T(8,128)(2,1)} %all-gather.12.cloned.1.call-done) | data formatting | bytes 5308416
  300.6 41.7 %collective-permute-done.5 = bf16[2,8,8,1152]{3,2,1,0:T(8,128)(2,1)} collective-permute-done((bf16[2,8,8,1152]{3,2,1,0:T(8,128)(2,1)S(1)}, bf16[2,8,8,1152]{3,2,1,0:T(8,128)(2,1)}, u32[]{:S(2)}, u32[]{:S(2)}) %collective-permute-start.5) | collective-permute-done | bytes 294944 | tf_op jit(solution)/shard_map/ppermute | solution.py:31
  343.4 3.7 conditional.8
  349.5 4.0 collective-permute-start.6
  358.7 4.0 collective-permute-start.9
  363.2 8.5 %collective-permute-start.8 = (bf16[2,20,6,1152]{3,0,2,1:T(2,128)(2,1)S(1)}, bf16[2,20,6,1152]{3,0,2,1:T(2,128)(2,1)S(1)}, u32[]{:S(2)}, u32[]{:S(2)}) collective-permute-start(bf16[2,20,6,1152]{3,0,2,1:T(2,128)(2,1)S(1)} %copy.78), channel_id=1, source_target_pairs={{0,1},{1,2},{2,3},{3,4},{4,5},{5,6},{6,7},{7,8},{8,9},{9,10},{10,1... | collective-permute-start | bytes 1658888 | tf_op jit(solution)/shard_map/ppermute | solution.py:20
  371.7 9.8 %collective-permute-done.9 = bf16[2,20,6,1152]{3,0,2,1:T(2,128)(2,1)S(1)} collective-permute-done((bf16[2,20,6,1152]{3,0,2,1:T(2,128)(2,1)S(1)}, bf16[2,20,6,1152]{3,0,2,1:T(2,128)(2,1)S(1)}, u32[]{:S(2)}, u32[]{:S(2)}) %collective-permute-start.9) | collective-permute-done | bytes 552992 | tf_op jit(solution)/shard_map/ppermute | solution.py:23
  381.7 3.1 pad_maximum_fusion.1
  384.8 24.9 %conditional.9 = (bf16[2,8,8,1152]{3,2,1,0:T(8,128)(2,1)}) conditional(s32[]{:T(128)} %convert_element_type.76, () %tuple.47, (f32[3,1152]{1,0:T(4,128)S(1)}, bf16[2,20,20,1152]{3,2,1,0:T(8,128)(2,1)}, s32[]{:T(128)}, s32[]{:T(128)}, bf16[128,576]{0,1:T(8,128)(2,1)S(1)}, /*index=5*/bf16[576,1152]{1,0:T(8,128)(2,1)S(1)}, ...), branch_computations={%region_14.15_spmd, %region_15.18_spmd} | conditional | flops 324553312 | bytes 28789580 | solution.py:155
  384.8 3.1 copy.82
  387.9 5.6 %pad_slice_fusion.2 = (bf16[2,512,576]{2,0,1:T(2,128)(2,1)S(1)}, bf16[2,512,576]{2,0,1:T(2,128)(2,1)}) fusion(bf16[2,400,1152]{2,0,1:T(2,128)(2,1)S(1)} %bitcast.91), kind=kLoop, calls=%fused_computation.55 | loop fusion | bytes 4202496 | tf_op jit(solution)/shard_map/cond/branch_1_fun/while/body/eval_jaxpr/slice | solution.py:88
  393.5 4.2 %copy.61 = bf16[2,512,576]{1,2,0:T(8,128)(2,1)} copy(bf16[2,512,576]{2,0,1:T(2,128)(2,1)} %get-tuple-element.221) | data formatting | bytes 2359296 | tf_op jit(solution)/shard_map/cond/branch_1_fun/while/body/eval_jaxpr/slice | solution.py:89
  398.4 3.1 copy.62
  402.4 3.6 fusion.41
  (89 shorter events, 52.4 us)
Async XLA Ops:
  6.5 13.8 %copy-start = (f32[2,3,1152]{2,0,1:T(2,128)S(1)}, f32[2,3,1152]{2,0,1:T(2,128)}, u32[]{:S(2)}) copy-start(f32[2,3,1152]{2,0,1:T(2,128)} %param.17) | copy-start | bytes 82948
  6.5 72.6 %all-gather.6.cloned.1.call-start = ((), (), s32[]{:S(2)}) async-start(), calls=%async_computation | async-start | bytes 2737152 | tf_op jit(solution)/shard_map/all_gather | solution.py:170
  8.1 142.8 %all-gather.8.cloned.1.call-start = ((), (), s32[]{:S(2)}) async-start(), calls=%async_computation.1 | async-start | bytes 5474304 | tf_op jit(solution)/shard_map/all_gather | solution.py:171
  9.8 211.8 %all-gather.10.cloned.1.call-start = ((), (), s32[]{:S(2)}) async-start(), calls=%async_computation.2 | async-start | bytes 2737152 | tf_op jit(solution)/shard_map/all_gather | solution.py:172
  11.4 276.4 %all-gather.12.cloned.1.call-start = ((), (), s32[]{:S(2)}) async-start(), calls=%async_computation.3 | async-start | bytes 3041280 | tf_op jit(solution)/shard_map/all_gather | solution.py:173
  12.0 14.3 %collective-permute-start = (bf16[2,8,8,1152]{3,2,1,0:T(8,128)(2,1)}, bf16[2,8,8,1152]{3,2,1,0:T(8,128)(2,1)S(1)}, u32[]{:S(2)}, u32[]{:S(2)}) collective-permute-start(bf16[2,8,8,1152]{3,2,1,0:T(8,128)(2,1)} %bitcast.100), channel_id=1, source_target_pairs={{0,256},{1,257},{2,258},{3,259},{4,260},{5,261},{6,262},{7,263},{8... | collective-permute-start | bytes 884744 | tf_op jit(solution)/shard_map/ppermute | solution.py:31
  162.6 1.1 copy-start.5
  163.7 8.6 %collective-permute-start.2 = (bf16[2,6,8,1152]{3,2,1,0:T(8,128)(2,1)S(1)}, bf16[2,6,8,1152]{3,2,1,0:T(8,128)(2,1)S(1)}, u32[]{:S(2)}, u32[]{:S(2)}) collective-permute-start(bf16[2,6,8,1152]{3,2,1,0:T(8,128)(2,1)S(1)} %get-tuple-element.235), channel_id=1, source_target_pairs={{32,0},{64,32},{96,64},{128,96},{160,128},{192,160},{224,192},{33,... | collective-permute-start | bytes 663560 | tf_op jit(solution)/shard_map/ppermute | solution.py:23
  165.0 8.2 %collective-permute-start.1 = (bf16[2,6,8,1152]{3,2,1,0:T(8,128)(2,1)S(1)}, bf16[2,6,8,1152]{3,2,1,0:T(8,128)(2,1)S(1)}, u32[]{:S(2)}, u32[]{:S(2)}) collective-permute-start(bf16[2,6,8,1152]{3,2,1,0:T(8,128)(2,1)S(1)} %get-tuple-element.234), channel_id=1, source_target_pairs={{0,32},{32,64},{64,96},{96,128},{128,160},{160,192},{192,224},{1,3... | collective-permute-start | bytes 663560 | tf_op jit(solution)/shard_map/ppermute | solution.py:20
  173.2 0.7 copy-start.3
  176.4 116.6 %collective-permute-start.4 = (bf16[2,20,6,1152]{3,0,2,1:T(2,128)(2,1)}, bf16[2,20,6,1152]{3,0,2,1:T(2,128)(2,1)}, u32[]{:S(2)}, u32[]{:S(2)}) collective-permute-start(bf16[2,20,6,1152]{3,0,2,1:T(2,128)(2,1)} %copy.70), channel_id=1, source_target_pairs={{1,0},{2,1},{3,2},{4,3},{5,4},{6,5},{7,6},{8,7},{9,8},{10,9},{11,1... | collective-permute-start | bytes 1658888 | tf_op jit(solution)/shard_map/ppermute | solution.py:23
  181.0 113.2 %collective-permute-start.3 = (bf16[2,20,6,1152]{3,0,2,1:T(2,128)(2,1)}, bf16[2,20,6,1152]{3,0,2,1:T(2,128)(2,1)}, u32[]{:S(2)}, u32[]{:S(2)}) collective-permute-start(bf16[2,20,6,1152]{3,0,2,1:T(2,128)(2,1)} %copy.69), channel_id=1, source_target_pairs={{0,1},{1,2},{2,3},{3,4},{4,5},{5,6},{6,7},{7,8},{8,9},{9,10},{10,1... | collective-permute-start | bytes 1658888 | tf_op jit(solution)/shard_map/ppermute | solution.py:20
  293.0 2.3 copy-start.4
  299.2 43.0 %collective-permute-start.5 = (bf16[2,8,8,1152]{3,2,1,0:T(8,128)(2,1)S(1)}, bf16[2,8,8,1152]{3,2,1,0:T(8,128)(2,1)}, u32[]{:S(2)}, u32[]{:S(2)}) collective-permute-start(bf16[2,8,8,1152]{3,2,1,0:T(8,128)(2,1)S(1)} %get-tuple-element.245), channel_id=1, source_target_pairs={{256,0},{257,1},{258,2},{259,3},{260,4},{261,5},{262,6},{263,7},{2... | collective-permute-start | bytes 884744 | tf_op jit(solution)/shard_map/ppermute | solution.py:31
  348.2 7.9 %collective-permute-start.7 = (bf16[2,6,8,1152]{3,2,1,0:T(8,128)(2,1)S(1)}, bf16[2,6,8,1152]{3,2,1,0:T(8,128)(2,1)S(1)}, u32[]{:S(2)}, u32[]{:S(2)}) collective-permute-start(bf16[2,6,8,1152]{3,2,1,0:T(8,128)(2,1)S(1)} %get-tuple-element.233), channel_id=1, source_target_pairs={{32,0},{64,32},{96,64},{128,96},{160,128},{192,160},{224,192},{33,... | collective-permute-start | bytes 663560 | tf_op jit(solution)/shard_map/ppermute | solution.py:23
  349.5 7.5 %collective-permute-start.6 = (bf16[2,6,8,1152]{3,2,1,0:T(8,128)(2,1)S(1)}, bf16[2,6,8,1152]{3,2,1,0:T(8,128)(2,1)S(1)}, u32[]{:S(2)}, u32[]{:S(2)}) collective-permute-start(bf16[2,6,8,1152]{3,2,1,0:T(8,128)(2,1)S(1)} %get-tuple-element.232), channel_id=1, source_target_pairs={{0,32},{32,64},{64,96},{96,128},{128,160},{160,192},{192,224},{1,3... | collective-permute-start | bytes 663560 | tf_op jit(solution)/shard_map/ppermute | solution.py:20
  358.7 22.8 %collective-permute-start.9 = (bf16[2,20,6,1152]{3,0,2,1:T(2,128)(2,1)S(1)}, bf16[2,20,6,1152]{3,0,2,1:T(2,128)(2,1)S(1)}, u32[]{:S(2)}, u32[]{:S(2)}) collective-permute-start(bf16[2,20,6,1152]{3,0,2,1:T(2,128)(2,1)S(1)} %copy.79), channel_id=1, source_target_pairs={{1,0},{2,1},{3,2},{4,3},{5,4},{6,5},{7,6},{8,7},{9,8},{10,9},{11,1... | collective-permute-start | bytes 1658888 | tf_op jit(solution)/shard_map/ppermute | solution.py:23
  363.2 18.4 %collective-permute-start.8 = (bf16[2,20,6,1152]{3,0,2,1:T(2,128)(2,1)S(1)}, bf16[2,20,6,1152]{3,0,2,1:T(2,128)(2,1)S(1)}, u32[]{:S(2)}, u32[]{:S(2)}) collective-permute-start(bf16[2,20,6,1152]{3,0,2,1:T(2,128)(2,1)S(1)} %copy.78), channel_id=1, source_target_pairs={{0,1},{1,2},{2,3},{3,4},{4,5},{5,6},{6,7},{7,8},{8,9},{9,10},{10,1... | collective-permute-start | bytes 1658888 | tf_op jit(solution)/shard_map/ppermute | solution.py:20
  381.7 3.1 copy-start.1
  384.8 8.7 %copy-start.7 = (bf16[128,576]{0,1:T(8,128)(2,1)}, bf16[128,576]{0,1:T(8,128)(2,1)S(1)}, u32[]{:S(2)}) copy-start(bf16[128,576]{0,1:T(8,128)(2,1)S(1)} %get-tuple-element.205) | copy-start | bytes 442372 | tf_op jit(solution)/shard_map/cond
  398.4 3.2 copy-start.8
  402.4 3.6 copy-start.2
Sparse Core Ops, SparseCore 0:
  9.5 69.5 all-gather.5
  81.3 69.5 all-gather.7
  153.1 68.5 all-gather.9
  223.7 64.0 all-gather.11
where the time goes:
time: 419 us; the launch traced here: 418 us
  waiting for transfers between devices  288 us (69%)
  local copies, waits for them, and re-layouts  55 us (13%)
  starting transfers between devices  38.7 us (9%)
  between operations  13.4 us (3%)
  other arithmetic  12.9 us (3%)
  matrix products  9.98 us (2%)
    all_gather x1, waiting for transfers between devices, on_device(): lax.all_gather(sources[1], 'tcol', axis=2, tiled=True)  68.8 us
    all_gather x1, waiting for transfers between devices, on_device(): lax.all_gather(w_zero, 'tcol', axis=1, tiled=True)  63.1 us
    all_gather x1, waiting for transfers between devices, on_device(): lax.all_gather(sources[0], 'tcol', axis=2, tiled=True)  51.8 us
    ppermute x2, waiting for transfers between devices, shifted(): return lax.ppermute(block, axis, route)  47.6 us
    all_gather x1, waiting for transfers between devices, on_device(): lax.all_gather(sources[2], 'tcol', axis=1, tiled=True)  38.2 us
    ppermute x4, starting transfers between devices, padded(): lax.ppermute(lax.slice_in_dim(block, block.shape[dim] - width, None, axis...  19.1 us
    unnamed x17, local copies, waits for them, and re-layouts  16.6 us
    ppermute x4, waiting for transfers between devices, padded(): lax.ppermute(lax.slice_in_dim(block, 0, width, axis=dim), axis, backward)  15.8 us
  transfers between devices with their start and end apart: 14, of which 11 were waited for; matrix products, arithmetic and copies ran while one was open for 8% of the time, Pallas kernels for 0%

commit v1 on v0

v1 whole, which is shorter than its diff:
```python
import math

import jax
import jax.numpy as jnp
from jax import lax
from jax.experimental import pallas as pl
from jax.experimental.pallas import tpu as pltpu
from jax.sharding import PartitionSpec as P

MESH = pl.DeviceIdType.MESH
F32 = jnp.float32
BF16 = jnp.bfloat16
D = 1152
HD = 72
GP = 24
HP = 96
NEG = -1e30
NT = (((1,), (1,)), ((), ()))
NN = (((1,), (0,)), ((), ()))


def dot(a, b, dims):
    return lax.dot_general(a, b, dims, preferred_element_type=F32)


def pick(rows, cols, pieces):
    r = lax.broadcasted_iota(jnp.int32, (rows, cols), 0)
    c = lax.broadcasted_iota(jnp.int32, (rows, cols), 1)
    hit = None
    for row0, col0, count in pieces:
        one = (r - row0 == c - col0) & (r >= row0) & (r < row0 + count)
        hit = one if hit is None else hit | one
    return jnp.where(hit, 1.0, 0.0).astype(BF16)


def kernel(
    lat, mod, wq, wkv, wo, wz, out,
    wb, g1, g0, gb, kvo, kvl, kvr, ob, ab, bias, hid, rlat, stage, q_s,
    lat_s, lat_r, w1y_s, w1x_s, w1s_s, w1_r, g1y_s, g1x_s, g1s_s, g1y_r, g1x_r, g1s_r,
    g0x_s, g0s_s, g0y_r, g0x_r, g0s_r, z_s, z_r, h_s, h_r, a_s, a_r, o_s, o_r,
):
    b = lax.axis_index("branch")
    z = lax.axis_index("trow")
    t = lax.axis_index("tcol")
    x, y, c = t // 8, (t // 2) % 4, t % 2
    yy = b * 4 + y
    partner = (1 - b, z, t)
    sibling = (b, z, t + 1 - 2 * c)
    left = (b, z, (t + 31) % 32)
    right = (b, z, (t + 1) % 32)
    column = []
    for k in range(1, 8):
        other = (yy + k) % 8
        column.append((other // 4, z, x * 8 + (other % 4) * 2 + c))
    line = [(b, z, ((x + k) % 4) * 8 + y * 2 + c) for k in range(1, 4)]
    ring = [(b, (z + k) % 8, t) for k in range(1, 8)]
    far = jnp.where(c == 0, (t + 31) % 32, (t + 1) % 32)

    def send(src, dst, ss, rs, dev):
        copy = pltpu.make_async_remote_copy(
            src_ref=src, dst_ref=dst, send_sem=ss, recv_sem=rs, device_id=dev, device_id_type=MESH
        )
        copy.start()
        return copy

    def arrived(dst, rs):
        pltpu.make_async_remote_copy(
            src_ref=dst, dst_ref=dst, send_sem=lat_s.at[0], recv_sem=rs, device_id=partner, device_id_type=MESH
        ).wait_recv()

    def sent(src, ss):
        pltpu.make_async_remote_copy(
            src_ref=src, dst_ref=src, send_sem=ss, recv_sem=lat_r.at[0], device_id=partner, device_id_type=MESH
        ).wait_send()

    barrier = pltpu.get_barrier_semaphore()
    for dev in column + line + ring + [sibling, (b, z, far)]:
        pl.semaphore_signal(barrier, inc=1, device_id=dev, device_id_type=MESH)

    rows = (
        dot(pick(144, 18, [(0, 0, 18)]), wq[...], NT)
        + dot(pick(144, 36, [(32, 0, 18), (56, 18, 18)]), wkv[...], NT)
        + dot(pick(144, 36, [(80, 0, 36)]), wz[...], NT)
        + dot(pick(144, 18, [(120, 0, 18)]), wo[...], NN)
    ).astype(BF16)
    own_q, own_kv = t // 4 == z, (t // 2) % 8 == z
    q_row = pl.multiple_of(32 * (t % 4), 16)
    kv_row = pl.multiple_of(128 + 96 * (t // 16) + 48 * c, 16)
    kv_idx = 4 + 2 * (t // 16) + c

    @pl.when(own_q)
    def _():
        wb[b, pl.ds(q_row, 32), :] = rows[0:32]

    @pl.when(own_kv)
    def _():
        wb[b, pl.ds(kv_row, 48), :] = rows[32:80]

    @pl.when(b == 1)
    def _():
        g1[c, x, y] = rows[80:144]

    @pl.when(b == 0)
    def _():
        g0[c, x, y] = jnp.concatenate(
            [rows[120:144].astype(F32), jnp.zeros((8, D), F32)], axis=0
        ).astype(BF16)

    pl.semaphore_wait(barrier, 19)

    lat_copy = send(lat.at[1 - b], rlat, lat_s.at[0], lat_r.at[0], partner)

    def w1_y(start):
        @pl.when(own_q)
        def _():
            piece = wb.at[b, pl.ds(q_row, 32)]
            for k in range(7):
                if start:
                    send(piece, piece, w1y_s.at[0, k], w1_r.at[b * 8 + t % 4], column[k])
                else:
                    sent(piece, w1y_s.at[0, k])

        @pl.when(own_kv)
        def _():
            piece = wb.at[b, pl.ds(kv_row, 48)]
            for k in range(7):
                if start:
                    send(piece, piece, w1y_s.at[1, k], w1_r.at[b * 8 + kv_idx], column[k])
                else:
                    sent(piece, w1y_s.at[1, k])

    def w2_y(start):
        @pl.when(b == 1)
        def _():
            piece = g1.at[c, x, y]
            for k in range(7):
                if start:
                    send(piece, piece, g1y_s.at[k], g1y_r.at[y], column[k])
                else:
                    sent(piece, g1y_s.at[k])

        @pl.when(b == 0)
        def _():
            piece = g0.at[c, x, y]
            for k in range(7):
                if start:
                    send(piece, piece, g1y_s.at[k], g0y_r.at[y], column[k])
                else:
                    sent(piece, g1y_s.at[k])

    w1_y(True)
    w2_y(True)

    for block in range(4):
        first, last = max(block - 1, 0), min(block + 1, 3)
        lanes = (last - first + 1) * 128
        q = lax.broadcasted_iota(jnp.int32, (128, lanes), 0)
        k = lax.broadcasted_iota(jnp.int32, (128, lanes), 1)
        i, j = block * 16 + q // 8, t * 8 + q % 8
        row, col = first * 16 + k // 8, (t - 1) * 8 + k % 8
        row0, col0 = jnp.clip(i - 6, 0, 51), jnp.clip(j - 6, 0, 243)
        row_ok = (row >= row0) & (row < row0 + 13)
        for strip in range(3):
            here = col + 8 * strip
            ok = row_ok & (here >= col0) & (here < col0 + 13)
            bias[block, :, strip * lanes : (strip + 1) * lanes] = jnp.where(ok, 0.0, NEG)
    ob[...] = jnp.zeros_like(ob)

    def normed(hidden, copy):
        average = jnp.mean(hidden, axis=-1, keepdims=True)
        centred = hidden - average
        variance = jnp.mean(centred * centred, axis=-1, keepdims=True)
        shift, scale = mod[copy, 0:1, :], mod[copy, 1:2, :]
        return (centred * lax.rsqrt(variance + 1e-06) * (1.0 + scale) + shift).astype(BF16)

    def slot(copy, index, half=None):
        start = 64 * ((index + 8) % 8)
        if half is None:
            return gb.at[copy, pl.ds(pl.multiple_of(start, 64), 64)]
        return gb.at[copy, pl.ds(pl.multiple_of(start + 32 * half, 32), 32)]

    def ring_step(copy, s):
        if s > 1:
            arrived(slot(copy, z - (s - 1)), z_r.at[copy, 0, s - 2])
        if s < 4:
            up = slot(copy, z - s + 1)
            down = slot(copy, z + s - 1)
        else:
            up = slot(copy, z - 3, 0)
            down = slot(copy, z + 3, 1)
        send(up, up, z_s.at[copy, 0, s - 1], z_r.at[copy, 0, s - 1], ring[0])
        if s > 1:
            arrived(slot(copy, z + (s - 1)), z_r.at[copy, 1, s - 2])
        send(down, down, z_s.at[copy, 1, s - 1], z_r.at[copy, 1, s - 1], ring[6])

    def ring_end(copy):
        arrived(slot(copy, z - 4, 0), z_r.at[copy, 0, 3])
        arrived(slot(copy, z + 4, 1), z_r.at[copy, 1, 3])

    def ring_sent(copy):
        for s in range(1, 4):
            sent(slot(copy, z - s + 1), z_s.at[copy, 0, s - 1])
            sent(slot(copy, z + s - 1), z_s.at[copy, 1, s - 1])
        sent(slot(copy, z - 3, 0), z_s.at[copy, 0, 3])
        sent(slot(copy, z + 3, 1), z_s.at[copy, 1, 3])

    def kinds(core):
        return (
            (32 * core, 32, core, 4 * z + core, z // 2),
            (32 * core + 64, 32, core + 2, 4 * z + core + 2, z // 2),
            (128 + 48 * core, 48, 4 + core, 2 * z + core, z // 4),
            (224 + 48 * core, 48, 6 + core, 16 + 2 * z + core, 2 + z // 4),
        )

    def w1_forward(copy):
        for n, (row, count, index, source, source_x) in enumerate(kinds(c)):
            piece = wb.at[copy, pl.ds(pl.multiple_of(row, 16), count)]

            @pl.when(jnp.logical_not((t == source) & (b == copy)))
            def _():
                arrived(piece, w1_r.at[copy * 8 + index])

            @pl.when(x == source_x)
            def _():
                for k in range(3):
                    send(piece, piece, w1x_s.at[copy, n, k], w1_r.at[copy * 8 + index], line[k])

            send(piece, piece, w1s_s.at[copy, n], w1_r.at[copy * 8 + index], sibling)

    def w1_end(copy):
        for row, count, index, source, source_x in kinds(1 - c):
            piece = wb.at[copy, pl.ds(pl.multiple_of(row, 16), count)]
            arrived(piece, w1_r.at[copy * 8 + index])

    def w1_sent(copy):
        for n, (row, count, index, source, source_x) in enumerate(kinds(c)):
            piece = wb.at[copy, pl.ds(pl.multiple_of(row, 16), count)]

            @pl.when(x == source_x)
            def _():
                for k in range(3):
                    sent(piece, w1x_s.at[copy, n, k])

            sent(piece, w1s_s.at[copy, n])

    def g1_line():
        for yk in range(4):
            piece = g1.at[c, x, yk]

            @pl.when(jnp.logical_not((b == 1) & (y == yk)))
            def _():
                arrived(piece, g1y_r.at[yk])

            for k in range(3):
                send(piece, piece, g1x_s.at[yk, k], g1x_r.at[x, yk], line[k])

    def g1_core():
        send(g1.at[c, x], g1.at[c, x], g1s_s.at[0], g1s_r.at[x], sibling)
        for k in range(1, 4):
            xk = (x + k) % 4
            for yk in range(4):
                arrived(g1.at[c, xk, yk], g1x_r.at[xk, yk])
            send(g1.at[c, xk], g1.at[c, xk], g1s_s.at[k], g1s_r.at[xk], sibling)

    def g1_end():
        for xk in range(4):
            arrived(g1.at[1 - c, xk], g1s_r.at[xk])

    def g1_sent():
        for yk in range(4):
            for k in range(3):
                sent(g1.at[c, x, yk], g1x_s.at[yk, k])
        for k in range(4):
            sent(g1.at[c, (x + k) % 4], g1s_s.at[k])

    def g0_line():
        for yk in range(4):

            @pl.when(jnp.logical_not((b == 0) & (y == yk)))
            def _():
                arrived(g0.at[c, x, yk], g0y_r.at[yk])

        for k in range(3):
            send(g0.at[c, x], g0.at[c, x], g0x_s.at[k], g0x_r.at[x], line[k])

    def g0_core():
        send(g0.at[c, x], g0.at[c, x], g0s_s.at[0], g0s_r.at[x], sibling)
        for k in range(1, 4):
            xk = (x + k) % 4
            arrived(g0.at[c, xk], g0x_r.at[xk])
            send(g0.at[c, xk], g0.at[c, xk], g0s_s.at[k], g0s_r.at[xk], sibling)

    def g0_end():
        for xk in range(4):
            arrived(g0.at[1 - c, xk], g0s_r.at[xk])

    def g0_sent():
        for k in range(3):
            sent(g0.at[c, x], g0x_s.at[k])
        for k in range(4):
            sent(g0.at[c, (x + k) % 4], g0s_s.at[k])

    def project(copy):
        w_q = jnp.concatenate(
            [wb[copy, 32 * n : 32 * n + 32, :].astype(F32)[0:GP] for n in range(4)], axis=0
        ).astype(BF16)
        tokens = gb[copy]
        kvo[copy] = dot(wb[copy, 128:320, :], tokens, NT).astype(BF16)
        send(kvo.at[copy], kvl.at[copy], h_s.at[copy, 0], h_r.at[copy, 0], right)
        send(kvo.at[copy], kvr.at[copy], h_s.at[copy, 1], h_r.at[copy, 1], left)
        q_s[...] = dot(tokens, w_q, NT).astype(BF16)

    def halo_end(copy):
        arrived(kvl.at[copy], h_r.at[copy, 0])
        arrived(kvr.at[copy], h_r.at[copy, 1])

    def attend(copy):
        for block in range(4):
            first, last = max(block - 1, 0), min(block + 1, 3)
            lanes = (last - first + 1) * 128
            span = slice(first * 128, first * 128 + lanes)
            keys = jnp.concatenate([ref[copy, 0:HP, span] for ref in (kvl, kvo, kvr)], axis=1)
            values = jnp.concatenate([ref[copy, HP : 2 * HP, span] for ref in (kvl, kvo, kvr)], axis=1)
            scores = dot(q_s[block * 128 : block * 128 + 128, :], keys, NN) * (1.0 / math.sqrt(HD))
            scores = scores + bias[block, :, 0 : 3 * lanes]
            raised = jnp.exp(scores - jnp.max(scores, axis=-1, keepdims=True))
            weights = (raised * (1.0 / jnp.sum(raised, axis=-1, keepdims=True))).astype(BF16)
            ob[copy, block * 128 : block * 128 + 128, 0:HP] = dot(weights, values, NT).astype(BF16)
            for tile in (2 * block, 2 * block + 1):

                @pl.when(z != tile)
                def _():
                    send(
                        ob.at[copy, pl.ds(64 * tile, 64)], ab.at[copy, z],
                        a_s.at[copy, tile], a_r.at[copy, z], (b, tile, t),
                    )

    def attended(copy):
        ab[copy, z] = ob[copy, pl.ds(pl.multiple_of(64 * z, 64), 64), :]
        for k in range(1, 8):
            head = (z + k) % 8
            arrived(ab.at[copy, head], a_r.at[copy, head])

    def attend_sent(copy):
        sent(kvo.at[copy], h_s.at[copy, 0])
        sent(kvo.at[copy], h_s.at[copy, 1])
        for tile in range(8):

            @pl.when(z != tile)
            def _():
                sent(ob.at[copy, pl.ds(64 * tile, 64)], a_s.at[copy, tile])

    def out_project(copy):
        total = jnp.zeros((64, D), F32)
        for head in range(8):
            parts = []
            for n in range(4):
                at = (n % 2, head // 2, 2 * (head % 2) + n // 2)
                if copy == 1:
                    parts.append(g1[at].astype(F32)[40:64])
                else:
                    parts.append(g0[at].astype(F32)[0:GP])
            w_head = jnp.concatenate(parts, axis=0).astype(BF16)
            total = total + dot(ab[copy, head][:, 0:HP], w_head, NN)
        return total

    def zero_project(control):
        parts = []
        for pair in range(16):
            two = [g1[core, pair // 4, pair % 4].astype(F32)[0:40] for core in range(2)]
            wide = dot(control, jnp.concatenate(two, axis=0).astype(BF16), NT)
            parts += [wide[:, 0:36], wide[:, 40:76]]
        return jnp.concatenate(parts, axis=1).astype(BF16)

    arrived(rlat, lat_r.at[0])
    mine, theirs = lat[b].astype(F32), rlat[...].astype(F32)
    control_in = mine + theirs
    hid[...] = control_in
    gb[1, pl.ds(pl.multiple_of(64 * z, 64), 64), :] = normed(control_in, 1)
    ring_step(1, 1)
    w1_forward(1)
    ring_step(1, 2)
    g1_line()
    ring_step(1, 3)
    w1_forward(0)
    ring_step(1, 4)
    w1_end(1)
    ring_end(1)
    project(1)
    g1_core()
    g0_line()
    halo_end(1)
    attend(1)
    g1_end()
    g0_core()
    attended(1)
    control = (hid[...] + mod[1, 2:3, :] * out_project(1)).astype(BF16)

    @pl.when(b == 0)
    def _():
        stage[...] = control
        send(stage, out.at[0], o_s.at[0], o_r.at[0], partner)

    @pl.when(b == 1)
    def _():
        out[1] = control

    residual = zero_project(control).astype(F32)
    base_in = jnp.where(b == 0, lat[b].astype(F32), rlat[...].astype(F32)) + residual
    hid[...] = base_in
    gb[0, pl.ds(pl.multiple_of(64 * z, 64), 64), :] = normed(base_in, 0)
    ring_step(0, 1)
    ring_step(0, 2)
    ring_step(0, 3)
    ring_step(0, 4)
    w1_end(0)
    ring_end(0)
    project(0)
    halo_end(0)
    attend(0)
    g0_end()
    attended(0)
    base = (hid[...] + mod[0, 2:3, :] * out_project(0)).astype(BF16)

    @pl.when(b == 1)
    def _():
        stage[...] = base
        send(stage, out.at[1], o_s.at[0], o_r.at[0], partner)

    @pl.when(b == 0)
    def _():
        out[0] = base

    lat_copy.wait_send()
    w1_y(False)
    w2_y(False)
    g1_sent()
    g0_sent()
    for copy in (1, 0):
        w1_sent(copy)
        ring_sent(copy)
        attend_sent(copy)
    sent(stage, o_s.at[0])
    arrived(out.at[1 - b], o_r.at[0])


def on_device(latent, modulation, w_query, w_keyval, w_out, w_zero):
    dma = pltpu.SemaphoreType.DMA
    vmem = pltpu.VMEM
    result = pl.pallas_call(
        kernel,
        out_shape=jax.ShapeDtypeStruct((2, 64, D), BF16),
        in_specs=[pl.BlockSpec(memory_space=pltpu.VMEM)] * 6,
        out_specs=pl.BlockSpec(memory_space=pltpu.VMEM),
        scratch_shapes=[
            vmem((2, 320, D), BF16),
            vmem((2, 4, 4, 64, D), BF16),
            vmem((2, 4, 4, 32, D), BF16),
            vmem((2, 512, D), BF16),
            vmem((2, 2 * HP, 512), BF16),
            vmem((2, 2 * HP, 512), BF16),
            vmem((2, 2 * HP, 512), BF16),
            vmem((2, 512, 128), BF16),
            vmem((2, 8, 64, 128), BF16),
            vmem((4, 128, D), F32),
            vmem((64, D), F32),
            vmem((64, D), BF16),
            vmem((64, D), BF16),
            vmem((512, HP), BF16),
            dma((1,)), dma((1,)),
            dma((2, 7)), dma((2, 4, 3)), dma((2, 4)), dma((16,)),
            dma((7,)), dma((4, 3)), dma((4,)), dma((4,)), dma((4, 4)), dma((4,)),
            dma((3,)), dma((4,)), dma((4,)), dma((4,)), dma((4,)),
            dma((2, 2, 4)), dma((2, 2, 4)), dma((2, 2)), dma((2, 2)),
            dma((2, 8)), dma((2, 8)), dma((1,)), dma((1,)),
        ],
        compiler_params=pltpu.CompilerParams(
            collective_id=0, has_side_effects=True, vmem_limit_bytes=56 * 1024 * 1024
        ),
    )(
        latent.reshape(2, 64, D), modulation, w_query[0], w_keyval[0], w_out[0], w_zero,
    )
    return result.reshape(latent.shape)


def solution(mesh):
    placed = (
        P("branch", None, "trow", "tcol", None),
        P(),
        P("branch", None, "tcol"),
        P("branch", None, "tcol"),
        P("branch", "tcol", None),
        P(None, "tcol"),
    )
    return jax.shard_map(
        on_device,
        mesh=mesh,
        in_specs=placed,
        out_specs=P("branch", None, "trow", "tcol", None),
        check_vma=False,
    )
```

time: 419 us -> 168 us (0.40)
  the two profiles are of different devices: /device:TPU:1 before, /device:TPU:9 now
where the time goes in v1:
time: 168 us; the launch traced here: 167 us
  Pallas kernels  161 us (96%)
  local copies, waits for them, and re-layouts  5.79 us (3%)
    pallas_call x1, Pallas kernels, on_device(): pl.pallas_call(kernel, out_shape=jax.ShapeDtypeStruct((2, 64, D), BF16),...  161 us
    unnamed x11, local copies, waits for them, and re-layouts  5.79 us

profile of v1, /device:TPU:9, one launch (start us, length us, event | category | flops | bytes accessed | tf_op | source)
XLA Modules:
  0.0 167.3 jit_solution(13932342405546570109)
XLA Ops:
  0.0 0.0 copy-start.2
  0.0 1.4 copy.9.mod
  1.4 0.0 copy-done.2
  1.4 0.0 copy-start
  1.4 0.9 copy.7
  2.3 0.0 copy-done
  2.3 0.0 copy-start.1
  2.3 0.9 copy.8
  3.2 0.0 copy-done.1
  3.2 0.9 copy.10.wz
  4.1 161.5 %shard_map.64 = bf16[2,64,1152]{2,1,0:T(8,128)(2,1)} custom-call(bf16[2,64,1152]{2,1,0:T(8,128)(2,1)} %bitcast.8, f32[2,3,1152]{2,1,0:T(4,128)} %copy.9.mod, bf16[1152,18]{1,0:T(8,128)(2,1)} %bitcast.6, bf16[1152,36]{1,0:T(8,128)(2,1)} %bitcast.7, bf16[18,1152]{1,0:T(8,128)(2,1)} %bitcast.9, bf16[1152,36]{1,0:T(8,128)(2,1)} %copy.10.wz), custom_call_target="tpu_custom_call" | custom-call | tf_op jit(solution)/shard_map/pallas_call | solution.py:450
  165.6 1.7 %copy.12 = bf16[1,2,8,8,1152]{4,3,2,1,0:T(8,128)(2,1)} copy(bf16[1,2,8,8,1152]{4,3,2,1,0:T(8,128)(2,1)} %bitcast.5) | data formatting | bytes 589824
Async XLA Ops:
  0.0 1.4 copy-start.2
  1.4 0.9 copy-start
  2.3 0.9 copy-start.1

commit v2 on v1

v2 whole, which is shorter than its diff:
```python
import math

import jax
import jax.numpy as jnp
from jax import lax
from jax.experimental import pallas as pl
from jax.experimental.pallas import tpu as pltpu
from jax.sharding import PartitionSpec as P

MESH = pl.DeviceIdType.MESH
F32 = jnp.float32
BF16 = jnp.bfloat16
D = 1152
HD = 72
GP = 24
HP = 96
NEG = -1e30
NT = (((1,), (1,)), ((), ()))
NN = (((1,), (0,)), ((), ()))


def dot(a, b, dims):
    return lax.dot_general(a, b, dims, preferred_element_type=F32)


def pick(rows, cols, pieces):
    r = lax.broadcasted_iota(jnp.int32, (rows, cols), 0)
    c = lax.broadcasted_iota(jnp.int32, (rows, cols), 1)
    hit = None
    for row0, col0, count in pieces:
        one = (r - row0 == c - col0) & (r >= row0) & (r < row0 + count)
        hit = one if hit is None else hit | one
    return jnp.where(hit, 1.0, 0.0).astype(BF16)


def kernel(
    lat_h, mod_h, wq_h, wkv_h, wo_h, wz_h, out,
    lat, mod, wq, wkv, wo, wz,
    wb, g1, g0, gb, kvo, kvl, kvr, ob, ab, ab0, bias, hid, rlat, rres, stage, res_s, q_s, wq_s,
    in_s, lat_s, lat_r, w1y_s, w1x_s, w1s_s, w1_r, g1y_s, g1x_s, g1s_s, g1y_r, g1x_r, g1s_r,
    g0y_s, g0x_s, g0s_s, g0y_r, g0x_r, g0s_r, z_s, z_r, h_s, h_r, a_s, a_r, a0_r, o_s, o_r, r_s, r_r,
):
    b = lax.axis_index("branch")
    z = lax.axis_index("trow")
    t = lax.axis_index("tcol")
    x, y, c = t // 8, (t // 2) % 4, t % 2
    yy = b * 4 + y
    partner = (1 - b, z, t)
    sibling = (b, z, t + 1 - 2 * c)
    left = (b, z, (t + 31) % 32)
    right = (b, z, (t + 1) % 32)
    column = []
    for k in range(1, 8):
        other = (yy + k) % 8
        column.append((other // 4, z, x * 8 + (other % 4) * 2 + c))
    line = [(b, z, ((x + k) % 4) * 8 + y * 2 + c) for k in range(1, 4)]
    ring = [(b, (z + k) % 8, t) for k in range(1, 8)]
    far = jnp.where(c == 0, (t + 31) % 32, (t + 1) % 32)

    def send(src, dst, ss, rs, dev):
        copy = pltpu.make_async_remote_copy(
            src_ref=src, dst_ref=dst, send_sem=ss, recv_sem=rs, device_id=dev, device_id_type=MESH
        )
        copy.start()
        return copy

    def arrived(dst, rs):
        pltpu.make_async_remote_copy(
            src_ref=dst, dst_ref=dst, send_sem=lat_s.at[0], recv_sem=rs, device_id=partner, device_id_type=MESH
        ).wait_recv()

    def sent(src, ss):
        pltpu.make_async_remote_copy(
            src_ref=src, dst_ref=src, send_sem=ss, recv_sem=lat_r.at[0], device_id=partner, device_id_type=MESH
        ).wait_send()

    barrier = pltpu.get_barrier_semaphore()
    across = [(1 - b, (z + k) % 8, t) for k in range(1, 8)]
    peers = column + line + ring + across + [sibling, (b, z, far)]
    for dev in peers:
        pl.semaphore_signal(barrier, inc=1, device_id=dev, device_id_type=MESH)

    loads = [
        pltpu.make_async_copy(src, dst, in_s.at[n])
        for n, (src, dst) in enumerate(
            ((wq_h, wq), (wkv_h, wkv), (wo_h, wo), (wz_h, wz), (lat_h, lat), (mod_h, mod))
        )
    ]
    for load in loads:
        load.start()
    for load in loads[:4]:
        load.wait()

    rows = (
        dot(pick(144, 18, [(0, 0, 18)]), wq[...], NN)
        + dot(pick(144, 36, [(32, 0, 18), (56, 18, 18)]), wkv[...], NN)
        + dot(pick(144, 36, [(80, 0, 36)]), wz[...], NN)
        + dot(pick(144, 18, [(120, 0, 18)]), wo[...], NN)
    ).astype(BF16)
    own_q, own_kv = t // 4 == z, (t // 2) % 8 == z
    q_row = pl.multiple_of(32 * (t % 4), 16)
    kv_row = pl.multiple_of(128 + 96 * (t // 16) + 48 * c, 16)
    kv_idx = 4 + 2 * (t // 16) + c

    @pl.when(own_q)
    def _():
        wb[b, pl.ds(q_row, 32), :] = rows[0:32]

    @pl.when(own_kv)
    def _():
        wb[b, pl.ds(kv_row, 48), :] = rows[32:80]

    @pl.when(b == 1)
    def _():
        g1[c, x, y] = rows[80:144]

    @pl.when(b == 0)
    def _():
        g0[c, x, y] = jnp.concatenate(
            [rows[120:144].astype(F32), jnp.zeros((8, D), F32)], axis=0
        ).astype(BF16)

    pl.semaphore_wait(barrier, len(peers))

    def lat_half(h):
        return send(
            lat_h.at[1 - b, pl.ds(32 * h, 32)], rlat.at[pl.ds(32 * h, 32)], lat_s.at[h], lat_r.at[h], partner
        )

    lat_copies = [lat_half(0), lat_half(1)]

    def w1_y(copy, start):
        @pl.when(own_q & (b == copy))
        def _():
            piece = wb.at[copy, pl.ds(q_row, 32)]
            for k in range(7):
                if start:
                    send(piece, piece, w1y_s.at[0, k], w1_r.at[copy * 8 + t % 4], column[k])
                else:
                    sent(piece, w1y_s.at[0, k])

        @pl.when(own_kv & (b == copy))
        def _():
            piece = wb.at[copy, pl.ds(kv_row, 48)]
            for k in range(7):
                if start:
                    send(piece, piece, w1y_s.at[1, k], w1_r.at[copy * 8 + kv_idx], column[k])
                else:
                    sent(piece, w1y_s.at[1, k])

    def g1_y(start):
        @pl.when(b == 1)
        def _():
            piece = g1.at[c, x, y]
            for k in range(7):
                if start:
                    send(piece, piece, g1y_s.at[k], g1y_r.at[y], column[k])
                else:
                    sent(piece, g1y_s.at[k])

    def g0_y(start):
        @pl.when(b == 0)
        def _():
            piece = g0.at[c, x, y]
            for k in range(1, 4):
                if start:
                    send(piece, piece, g0y_s.at[k - 1], g0y_r.at[y], (b, z, x * 8 + ((y + k) % 4) * 2 + c))
                else:
                    sent(piece, g0y_s.at[k - 1])

    w1_y(1, True)

    for block in range(4):
        first, last = max(block - 1, 0), min(block + 1, 3)
        lanes = (last - first + 1) * 128
        q = lax.broadcasted_iota(jnp.int32, (128, lanes), 0)
        k = lax.broadcasted_iota(jnp.int32, (128, lanes), 1)
        i, j = block * 16 + q // 8, t * 8 + q % 8
        row, col = first * 16 + k // 8, (t - 1) * 8 + k % 8
        row0, col0 = jnp.clip(i - 6, 0, 51), jnp.clip(j - 6, 0, 243)
        row_ok = (row >= row0) & (row < row0 + 13)
        for strip in range(3):
            here = col + 8 * strip
            ok = row_ok & (here >= col0) & (here < col0 + 13)
            bias[block, :, strip * lanes : (strip + 1) * lanes] = jnp.where(ok, 0.0, NEG)
    ob[...] = jnp.zeros_like(ob)

    def normed(hidden, copy):
        average = jnp.mean(hidden, axis=-1, keepdims=True)
        centred = hidden - average
        variance = jnp.mean(centred * centred, axis=-1, keepdims=True)
        shift, scale = mod[0, copy : copy + 1, :], mod[1, copy : copy + 1, :]
        return (centred * lax.rsqrt(variance + 1e-06) * (1.0 + scale) + shift).astype(BF16)

    def half_tile(copy, index, h):
        start = 64 * ((index + 8) % 8) + 32 * h
        return gb.at[copy, pl.ds(pl.multiple_of(start, 32), 32)]

    def ring_send(copy, s, way, h):
        tile = half_tile(copy, z - s + 1 if way == 0 else z + s - 1, h)
        send(tile, tile, z_s.at[copy, way, s - 1, h], z_r.at[copy, way, s - 1, h], ring[0] if way == 0 else ring[6])

    def ring_take(copy, s, way, h):
        arrived(half_tile(copy, z - s if way == 0 else z + s, h), z_r.at[copy, way, s - 1, h])

    def ring_start(copy, h):
        ring_send(copy, 1, 0, h)
        ring_send(copy, 1, 1, h)

    def ring_step(copy, s):
        for h in range(2):
            for way in range(2):
                ring_take(copy, s - 1, way, h)
                if s < 4 or h == way:
                    ring_send(copy, s, way, h)

    def ring_end(copy):
        ring_take(copy, 4, 0, 0)
        ring_take(copy, 4, 1, 1)

    def ring_sent(copy):
        for s in range(1, 5):
            for h in range(2):
                for way in range(2):
                    if s < 4 or h == way:
                        sent(half_tile(copy, z, h), z_s.at[copy, way, s - 1, h])

    def kinds(core):
        return (
            (32 * core, 32, core, 4 * z + core, z // 2),
            (32 * core + 64, 32, core + 2, 4 * z + core + 2, z // 2),
            (128 + 48 * core, 48, 4 + core, 2 * z + core, z // 4),
            (224 + 48 * core, 48, 6 + core, 16 + 2 * z + core, 2 + z // 4),
        )

    def w1_forward(copy):
        for n, (row, count, index, source, source_x) in enumerate(kinds(c)):
            piece = wb.at[copy, pl.ds(pl.multiple_of(row, 16), count)]

            @pl.when(jnp.logical_not((t == source) & (b == copy)))
            def _():
                arrived(piece, w1_r.at[copy * 8 + index])

            @pl.when(x == source_x)
            def _():
                for k in range(3):
                    send(piece, piece, w1x_s.at[copy, n, k], w1_r.at[copy * 8 + index], line[k])

            send(piece, piece, w1s_s.at[copy, n], w1_r.at[copy * 8 + index], sibling)

    def w1_end(copy):
        for row, count, index, source, source_x in kinds(1 - c):
            piece = wb.at[copy, pl.ds(pl.multiple_of(row, 16), count)]
            arrived(piece, w1_r.at[copy * 8 + index])

    def w1_sent(copy):
        for n, (row, count, index, source, source_x) in enumerate(kinds(c)):
            piece = wb.at[copy, pl.ds(pl.multiple_of(row, 16), count)]

            @pl.when(x == source_x)
            def _():
                for k in range(3):
                    sent(piece, w1x_s.at[copy, n, k])

            sent(piece, w1s_s.at[copy, n])

    def g1_line(k):
        yk = (y + k) % 4
        piece = g1.at[c, x, yk]
        if k == 0:

            @pl.when(b == 0)
            def _():
                arrived(piece, g1y_r.at[yk])
        else:
            arrived(piece, g1y_r.at[yk])
        for n in range(3):
            send(piece, piece, g1x_s.at[k, n], g1x_r.at[x, yk], line[n])

    def g1_core():
        send(g1.at[c, x], g1.at[c, x], g1s_s.at[0], g1s_r.at[x], sibling)
        for k in range(1, 4):
            xk = (x + k) % 4
            for yk in range(4):
                arrived(g1.at[c, xk, yk], g1x_r.at[xk, yk])
            send(g1.at[c, xk], g1.at[c, xk], g1s_s.at[k], g1s_r.at[xk], sibling)

    def g1_end():
        for xk in range(4):
            arrived(g1.at[1 - c, xk], g1s_r.at[xk])

    def g1_sent():
        for yk in range(4):
            for k in range(3):
                sent(g1.at[c, x, yk], g1x_s.at[yk, k])
        for k in range(4):
            sent(g1.at[c, (x + k) % 4], g1s_s.at[k])

    def g0_line():
        for k in range(1, 4):
            yk = (y + k) % 4
            arrived(g0.at[c, x, yk], g0y_r.at[yk])
        for k in range(3):
            send(g0.at[c, x], g0.at[c, x], g0x_s.at[k], g0x_r.at[x], line[k])
        send(g0.at[c, x], g0.at[c, x], g0s_s.at[0], g0s_r.at[x], sibling)

    def g0_core():
        for k in range(1, 4):
            xk = (x + k) % 4
            arrived(g0.at[c, xk], g0x_r.at[xk])
            send(g0.at[c, xk], g0.at[c, xk], g0s_s.at[k], g0s_r.at[xk], sibling)

    def g0_end():
        for xk in range(4):
            arrived(g0.at[1 - c, xk], g0s_r.at[xk])

    def g0_sent():
        for k in range(3):
            sent(g0.at[c, x], g0x_s.at[k])
        for k in range(4):
            sent(g0.at[c, (x + k) % 4], g0s_s.at[k])

    side = 1 - 2 * (z % 2)
    order = [z // 2, (z // 2 + 4 - side) % 4, (z // 2 + 4 + side) % 4, (z // 2 + 2) % 4]

    def pack_query(copy):
        wq_s[...] = jnp.concatenate(
            [wb[copy, 32 * n : 32 * n + 32, :].astype(F32)[0:GP] for n in range(4)], axis=0
        ).astype(BF16)

    def project(copy, s):
        pair = order[s - 1]
        span = pl.ds(pl.multiple_of(128 * pair, 128), 128)
        tokens = gb[copy, span, :]
        kvo[copy, pair] = dot(wb[copy, 128:320, :], tokens, NT).astype(BF16)
        send(kvo.at[copy, pair], kvl.at[copy, pair], h_s.at[copy, 0, s - 1], h_r.at[copy, 0, s - 1], right)
        send(kvo.at[copy, pair], kvr.at[copy, pair], h_s.at[copy, 1, s - 1], h_r.at[copy, 1, s - 1], left)
        q_s[span, :] = dot(tokens, wq_s[...], NT).astype(BF16)

    def halo_end(copy):
        for s in range(4):
            arrived(kvl.at[copy, order[s]], h_r.at[copy, 0, s])
            arrived(kvr.at[copy, order[s]], h_r.at[copy, 1, s])

    def attend(copy):
        for block in range(4):
            first, last = max(block - 1, 0), min(block + 1, 3)
            lanes = (last - first + 1) * 128
            pieces = [ref[copy, n] for ref in (kvl, kvo, kvr) for n in range(first, last + 1)]
            keys = jnp.concatenate([piece[0:HP] for piece in pieces], axis=1)
            values = jnp.concatenate([piece[HP : 2 * HP] for piece in pieces], axis=1)
            scores = dot(q_s[block * 128 : block * 128 + 128, :], keys, NN) * (1.0 / math.sqrt(HD))
            scores = scores + bias[block, :, 0 : 3 * lanes]
            raised = jnp.exp(scores - jnp.max(scores, axis=-1, keepdims=True))
            weights = (raised * (1.0 / jnp.sum(raised, axis=-1, keepdims=True))).astype(BF16)
            ob[copy, block * 128 : block * 128 + 128, 0:HP] = dot(weights, values, NT).astype(BF16)
            for tile in (2 * block, 2 * block + 1):
                piece = ob.at[copy, pl.ds(64 * tile, 64)]
                if copy == 1:

                    @pl.when(z != tile)
                    def _():
                        send(piece, ab.at[z], a_s.at[copy, tile], a_r.at[z], (b, tile, t))
                else:

                    @pl.when((z != tile) | (b == 1))
                    def _():
                        send(piece, ab0.at[b, z], a_s.at[copy, tile], a0_r.at[b, z], (0, tile, t))

    def own_tile(copy):
        return ob[copy, pl.ds(pl.multiple_of(64 * z, 64), 64), :]

    def attended():
        ab[z] = own_tile(1)
        for k in range(1, 8):
            head = (z + k) % 8
            arrived(ab.at[head], a_r.at[head])

    def attended_base():
        ab0[0, z] = own_tile(0)
        for k in range(8):
            head = (z + k) % 8
            if k > 0:
                arrived(ab0.at[0, head], a0_r.at[0, head])
            arrived(ab0.at[1, head], a0_r.at[1, head])

    def attend_sent(copy):
        for s in range(4):
            sent(kvo.at[copy, order[s]], h_s.at[copy, 0, s])
            sent(kvo.at[copy, order[s]], h_s.at[copy, 1, s])
        for tile in range(8):

            @pl.when((z != tile) | ((b == 1) & (copy == 0)))
            def _():
                sent(ob.at[copy, pl.ds(64 * tile, 64)], a_s.at[copy, tile])

    def out_project(copy):
        total = None
        for head in range(8):
            parts = []
            for n in range(4):
                at = (n % 2, head // 2, 2 * (head % 2) + n // 2)
                if copy == 1:
                    parts.append(g1[at].astype(F32)[40:64])
                else:
                    parts.append(g0[at].astype(F32)[0:GP])
            w_head = jnp.concatenate(parts, axis=0).astype(BF16)
            if copy == 1:
                mixed = ab[head][:, 0:HP]
            else:
                mixed = jnp.concatenate([ab0[0, head][:, 0:HP], ab0[1, head][:, 0:HP]], axis=0)
            part = dot(mixed, w_head, NN)
            total = part if total is None else total + part
        return total

    def zero_project(control):
        parts = []
        for pair in range(16):
            two = [g1[core, pair // 4, pair % 4].astype(F32)[0:40] for core in range(2)]
            wide = dot(control, jnp.concatenate(two, axis=0).astype(BF16), NT)
            parts += [wide[:, 0:36], wide[:, 40:76]]
        return jnp.concatenate(parts, axis=1).astype(BF16)

    for load in loads[4:]:
        load.wait()
    for h in range(2):
        part = pl.ds(32 * h, 32)
        arrived(rlat.at[part], lat_r.at[h])
        control_in = lat[b, part, :].astype(F32) + rlat[part, :].astype(F32)
        hid[part, :] = control_in
        gb[1, pl.ds(pl.multiple_of(64 * z + 32 * h, 32), 32), :] = normed(control_in, 1)
        ring_start(1, h)
    w1_forward(1)
    g1_y(True)

    @pl.when(b == 1)
    def _():
        g1_line(0)

    ring_step(1, 2)
    w1_end(1)
    pack_query(1)
    project(1, 1)
    ring_step(1, 3)
    project(1, 2)
    ring_step(1, 4)
    project(1, 3)
    ring_end(1)
    project(1, 4)
    g1_line(1)
    g1_line(2)
    g1_line(3)

    @pl.when(b == 0)
    def _():
        g1_line(0)

    w1_y(0, True)
    halo_end(1)
    attend(1)
    w1_forward(0)
    g1_core()
    g0_y(True)
    attended()
    g1_end()
    control = (hid[...] + mod[2, 1:2, :] * out_project(1)).astype(BF16)

    @pl.when(b == 0)
    def _():
        stage[...] = control
        send(stage, out.at[0], o_s.at[0], o_r.at[0], partner)

    @pl.when(b == 1)
    def _():
        out[1] = control

    residual = zero_project(control)
    base_in = jnp.where(b == 0, lat[b].astype(F32), rlat[...].astype(F32)) + residual.astype(F32)
    hid[...] = base_in
    gb[0, pl.ds(pl.multiple_of(64 * z, 64), 64), :] = normed(base_in, 0)
    ring_start(0, 0)
    ring_start(0, 1)

    @pl.when(b == 1)
    def _():
        res_s[...] = residual
        send(res_s, rres, r_s.at[0], r_r.at[0], partner)

    w1_end(0)
    pack_query(0)
    ring_step(0, 2)
    project(0, 1)
    ring_step(0, 3)
    project(0, 2)
    ring_step(0, 4)
    project(0, 3)
    ring_end(0)
    project(0, 4)

    @pl.when(b == 0)
    def _():
        g0_line()

    halo_end(0)
    attend(0)

    @pl.when(b == 0)
    def _():
        g0_core()
        arrived(rres, r_r.at[0])
        attended_base()
        g0_end()
        second = lat[1].astype(F32) + rres[...].astype(F32)
        gated = mod[2, 0:1, :] * out_project(0)
        out[0] = (hid[...] + gated[0:64]).astype(BF16)
        out[1] = (second + gated[64:128]).astype(BF16)
        sent(stage, o_s.at[0])
        g0_sent()

    @pl.when(b == 1)
    def _():
        arrived(out.at[0], o_r.at[0])
        sent(res_s, r_s.at[0])

    for copy in lat_copies:
        copy.wait_send()
    g1_y(False)
    g0_y(False)
    g1_sent()
    for copy in (1, 0):
        w1_y(copy, False)
        w1_sent(copy)
        ring_sent(copy)
        attend_sent(copy)


def on_device(latent, modulation, w_query, w_keyval, w_out, w_zero):
    dma = pltpu.SemaphoreType.DMA
    vmem = pltpu.VMEM
    result = pl.pallas_call(
        kernel,
        out_shape=jax.ShapeDtypeStruct((2, 64, D), BF16),
        in_specs=[pl.BlockSpec(memory_space=pl.ANY)] * 6,
        out_specs=pl.BlockSpec(memory_space=pltpu.VMEM),
        scratch_shapes=[
            vmem((2, 64, D), BF16),
            vmem((3, 2, D), F32),
            vmem((18, D), BF16),
            vmem((36, D), BF16),
            vmem((18, D), BF16),
            vmem((36, D), BF16),
            vmem((2, 320, D), BF16),
            vmem((2, 4, 4, 64, D), BF16),
            vmem((2, 4, 4, 32, D), BF16),
            vmem((2, 512, D), BF16),
            vmem((2, 4, 2 * HP, 128), BF16),
            vmem((2, 4, 2 * HP, 128), BF16),
            vmem((2, 4, 2 * HP, 128), BF16),
            vmem((2, 512, 128), BF16),
            vmem((8, 64, 128), BF16),
            vmem((2, 8, 64, 128), BF16),
            vmem((4, 128, D), F32),
            vmem((64, D), F32),
            vmem((64, D), BF16),
            vmem((64, D), BF16),
            vmem((64, D), BF16),
            vmem((64, D), BF16),
            vmem((512, HP), BF16),
            vmem((HP, D), BF16),
            dma((6,)), dma((2,)), dma((2,)),
            dma((2, 7)), dma((2, 4, 3)), dma((2, 4)), dma((16,)),
            dma((7,)), dma((4, 3)), dma((4,)), dma((4,)), dma((4, 4)), dma((4,)),
            dma((3,)), dma((3,)), dma((4,)), dma((4,)), dma((4,)), dma((4,)),
            dma((2, 2, 4, 2)), dma((2, 2, 4, 2)), dma((2, 2, 4)), dma((2, 2, 4)),
            dma((2, 8)), dma((8,)), dma((2, 8)), dma((1,)), dma((1,)), dma((1,)), dma((1,)),
        ],
        compiler_params=pltpu.CompilerParams(
            collective_id=0, has_side_effects=True, vmem_limit_bytes=56 * 1024 * 1024
        ),
    )(
        latent.reshape(2, 64, D), modulation.swapaxes(0, 1), w_query[0].T, w_keyval[0].T, w_out[0], w_zero.T,
    )
    return result.reshape(latent.shape)


def solution(mesh):
    placed = (
        P("branch", None, "trow", "tcol", None),
        P(),
        P("branch", None, "tcol"),
        P("branch", None, "tcol"),
        P("branch", "tcol", None),
        P(None, "tcol"),
    )
    return jax.shard_map(
        on_device,
        mesh=mesh,
        in_specs=placed,
        out_specs=P("branch", None, "trow", "tcol", None),
        check_vma=False,
    )
```

time: 168 us -> 155 us (0.923)
  the two profiles are of different devices: /device:TPU:9 before, /device:TPU:21 now
where the time goes in v2:
time: 155 us
  Pallas kernels  153 us (99%)
  local copies, waits for them, and re-layouts  1.7 us (1%)
    pallas_call x1, Pallas kernels, on_device(): pl.pallas_call(kernel, out_shape=jax.ShapeDtypeStruct((2, 64, D), BF16),...  153 us

profile of v2, /device:TPU:21, one launch (start us, length us, event | category | flops | bytes accessed | tf_op | source)
XLA Modules:
  0.0 154.6 jit_solution(10002448855263659524)
XLA Ops:
  0.0 152.9 %shard_map.64 = bf16[2,64,1152]{2,1,0:T(8,128)(2,1)} custom-call(bf16[2,64,1152]{2,1,0:T(8,128)(2,1)} %bitcast.12, f32[3,2,1152]{2,1,0:T(2,128)} %bitcast.17, bf16[18,1152]{1,0:T(8,128)(2,1)} %bitcast.15, bf16[36,1152]{1,0:T(8,128)(2,1)} %bitcast.13, bf16[18,1152]{1,0:T(8,128)(2,1)} %bitcast.16, bf16[36,1152]{1,0:T(8,128)(2,1)} %bitcast.14), custom_call_target="tpu_custom_call" | custom-call | tf_op jit(solution)/shard_map/pallas_call | solution.py:540
  152.9 1.7 %copy.8 = bf16[1,2,8,8,1152]{4,3,2,1,0:T(8,128)(2,1)} copy(bf16[1,2,8,8,1152]{4,3,2,1,0:T(8,128)(2,1)} %bitcast.11) | data formatting | bytes 589824

commit v3 on v2

--- a/solution.py
+++ b/solution.py
@@ -37,7 +37,7 @@
     lat_h, mod_h, wq_h, wkv_h, wo_h, wz_h, out,
     lat, mod, wq, wkv, wo, wz,
     wb, g1, g0, gb, kvo, kvl, kvr, ob, ab, ab0, bias, hid, rlat, rres, stage, res_s, q_s, wq_s,
-    in_s, lat_s, lat_r, w1y_s, w1x_s, w1s_s, w1_r, g1y_s, g1x_s, g1s_s, g1y_r, g1x_r, g1s_r,
+    in_s, lat_s, lat_r, w1y_s, w1t_s, w1x_s, w1s_s, w1_r, g1y_s, g1x_s, g1s_s, g1y_r, g1x_r, g1s_r,
     g0y_s, g0x_s, g0s_s, g0y_r, g0x_r, g0s_r, z_s, z_r, h_s, h_r, a_s, a_r, a0_r, o_s, o_r, r_s, r_r,
 ):
     b = lax.axis_index("branch")
@@ -133,30 +133,20 @@
         @pl.when(own_q & (b == copy))
         def _():
             piece = wb.at[copy, pl.ds(q_row, 32)]
-            for k in range(7):
+            for n, k in enumerate((2, 6, 1, 7)):
                 if start:
-                    send(piece, piece, w1y_s.at[0, k], w1_r.at[copy * 8 + t % 4], column[k])
+                    send(piece, piece, w1y_s.at[0, n], w1_r.at[copy * 8 + t % 4], column[k - 1])
                 else:
-                    sent(piece, w1y_s.at[0, k])
+                    sent(piece, w1y_s.at[0, n])
 
         @pl.when(own_kv & (b == copy))
         def _():
             piece = wb.at[copy, pl.ds(kv_row, 48)]
-            for k in range(7):
+            for n, k in enumerate((2, 6, 1, 7)):
                 if start:
-                    send(piece, piece, w1y_s.at[1, k], w1_r.at[copy * 8 + kv_idx], column[k])
+                    send(piece, piece, w1y_s.at[1, n], w1_r.at[copy * 8 + kv_idx], column[k - 1])
                 else:
-                    sent(piece, w1y_s.at[1, k])
-
-    def g1_y(start):
-        @pl.when(b == 1)
-        def _():
-            piece = g1.at[c, x, y]
-            for k in range(7):
-                if start:
-                    send(piece, piece, g1y_s.at[k], g1y_r.at[y], column[k])
-                else:
-                    sent(piece, g1y_s.at[k])
+                    sent(piece, w1y_s.at[1, n])
 
     def g0_y(start):
         @pl.when(b == 0)
@@ -233,20 +223,45 @@
             (224 + 48 * core, 48, 6 + core, 16 + 2 * z + core, 2 + z // 4),
         )
 
-    def w1_forward(copy):
+    def w1_tree(copy, start):
         for n, (row, count, index, source, source_x) in enumerate(kinds(c)):
             piece = wb.at[copy, pl.ds(pl.multiple_of(row, 16), count)]
-
-            @pl.when(jnp.logical_not((t == source) & (b == copy)))
+            away = (yy + 8 - (copy * 4 + (source // 2) % 4)) % 8
+            for here, steps in ((2, (2, 1)), (6, (7,))):
+
+                @pl.when((x == source_x) & (away == here))
+                def _():
+                    if start:
+                        arrived(piece, w1_r.at[copy * 8 + index])
+                    for m, k in enumerate(steps):
+                        if start:
+                            send(piece, piece, w1t_s.at[copy, n, m], w1_r.at[copy * 8 + index], column[k - 1])
+                        else:
+                            sent(piece, w1t_s.at[copy, n, m])
+
+    def w1_line(copy):
+        for n, (row, count, index, source, source_x) in enumerate(kinds(c)):
+            piece = wb.at[copy, pl.ds(pl.multiple_of(row, 16), count)]
+            away = (yy + 8 - (copy * 4 + (source // 2) % 4)) % 8
+
+            @pl.when(x == source_x)
+            def _():
+                @pl.when((away != 0) & (away != 2) & (away != 6))
+                def _():
+                    arrived(piece, w1_r.at[copy * 8 + index])
+
+                for k in range(3):
+                    send(piece, piece, w1x_s.at[copy, n, k], w1_r.at[copy * 8 + index], line[k])
+                send(piece, piece, w1s_s.at[copy, n], w1_r.at[copy * 8 + index], sibling)
+
+    def w1_core(copy):
+        for n, (row, count, index, source, source_x) in enumerate(kinds(c)):
+            piece = wb.at[copy, pl.ds(pl.multiple_of(row, 16), count)]
+
+            @pl.when(x != source_x)
             def _():
                 arrived(piece, w1_r.at[copy * 8 + index])
-
-            @pl.when(x == source_x)
-            def _():
-                for k in range(3):
-                    send(piece, piece, w1x_s.at[copy, n, k], w1_r.at[copy * 8 + index], line[k])
-
-            send(piece, piece, w1s_s.at[copy, n], w1_r.at[copy * 8 + index], sibling)
+                send(piece, piece, w1s_s.at[copy, n], w1_r.at[copy * 8 + index], sibling)
 
     def w1_end(copy):
         for row, count, index, source, source_x in kinds(1 - c):
@@ -264,18 +279,41 @@
 
             sent(piece, w1s_s.at[copy, n])
 
-    def g1_line(k):
-        yk = (y + k) % 4
-        piece = g1.at[c, x, yk]
-        if k == 0:
-
-            @pl.when(b == 0)
-            def _():
-                arrived(piece, g1y_r.at[yk])
-        else:
-            arrived(piece, g1y_r.at[yk])
+    def g1_line(yk):
         for n in range(3):
-            send(piece, piece, g1x_s.at[k, n], g1x_r.at[x, yk], line[n])
+            send(g1.at[c, x, yk], g1.at[c, x, yk], g1x_s.at[yk, n], g1x_r.at[x, yk], line[n])
+
+    def g1_send(s, way):
+        at = (yy + 9 - s if way == 0 else yy + s - 1) % 8
+        piece = g1.at[c, x, at % 4]
+
+        @pl.when(at >= 4)
+        def _():
+            send(piece, piece, g1y_s.at[way, s - 1], g1y_r.at[at % 4], column[0 if way == 0 else 6])
+
+    def g1_take(s, way):
+        at = (yy + 8 - s if way == 0 else yy + s) % 8
+
+        @pl.when(at >= 4)
+        def _():
+            arrived(g1.at[c, x, at % 4], g1y_r.at[at % 4])
+            if s < (4 if way == 0 else 3):
+                g1_pass(s + 1, way)
+            g1_line(at % 4)
+
+    def g1_pass(s, way):
+        at = (yy + 9 - s if way == 0 else yy + s - 1) % 8
+        piece = g1.at[c, x, at % 4]
+        send(piece, piece, g1y_s.at[way, s - 1], g1y_r.at[at % 4], column[0 if way == 0 else 6])
+
+    def g1_y_sent():
+        for way in range(2):
+            for s in range(1, 5 - way):
+                at = (yy + 9 - s if way == 0 else yy + s - 1) % 8
+
+                @pl.when(at >= 4)
+                def _():
+                    sent(g1.at[c, x, at % 4], g1y_s.at[way, s - 1])
 
     def g1_core():
         send(g1.at[c, x], g1.at[c, x], g1s_s.at[0], g1s_r.at[x], sibling)
@@ -430,35 +468,36 @@
         hid[part, :] = control_in
         gb[1, pl.ds(pl.multiple_of(64 * z + 32 * h, 32), 32), :] = normed(control_in, 1)
         ring_start(1, h)
-    w1_forward(1)
-    g1_y(True)
+
+    w1_tree(1, True)
+    g1_send(1, 0)
+    g1_send(1, 1)
 
     @pl.when(b == 1)
     def _():
-        g1_line(0)
+        g1_line(y)
 
     ring_step(1, 2)
+    w1_line(1)
+    g1_take(1, 0)
+    g1_take(1, 1)
+    ring_step(1, 3)
+    g1_take(2, 0)
+    g1_take(2, 1)
+    ring_step(1, 4)
+    ring_end(1)
+    w1_core(1)
     w1_end(1)
     pack_query(1)
-    project(1, 1)
-    ring_step(1, 3)
-    project(1, 2)
-    ring_step(1, 4)
-    project(1, 3)
-    ring_end(1)
-    project(1, 4)
-    g1_line(1)
-    g1_line(2)
-    g1_line(3)
-
-    @pl.when(b == 0)
-    def _():
-        g1_line(0)
-
+    for s in range(1, 5):
+        project(1, s)
+    g1_take(3, 0)
+    g1_take(3, 1)
     w1_y(0, True)
     halo_end(1)
     attend(1)
-    w1_forward(0)
+    g1_take(4, 0)
+    w1_tree(0, True)
     g1_core()
     g0_y(True)
     attended()
@@ -480,15 +519,17 @@
     gb[0, pl.ds(pl.multiple_of(64 * z, 64), 64), :] = normed(base_in, 0)
     ring_start(0, 0)
     ring_start(0, 1)
+    w1_line(0)
 
     @pl.when(b == 1)
     def _():
         res_s[...] = residual
         send(res_s, rres, r_s.at[0], r_r.at[0], partner)
 
+    ring_step(0, 2)
+    w1_core(0)
     w1_end(0)
     pack_query(0)
-    ring_step(0, 2)
     project(0, 1)
     ring_step(0, 3)
     project(0, 2)
@@ -524,11 +565,12 @@
 
     for copy in lat_copies:
         copy.wait_send()
-    g1_y(False)
+    g1_y_sent()
     g0_y(False)
     g1_sent()
     for copy in (1, 0):
         w1_y(copy, False)
+        w1_tree(copy, False)
         w1_sent(copy)
         ring_sent(copy)
         attend_sent(copy)
@@ -568,8 +610,8 @@
             vmem((512, HP), BF16),
             vmem((HP, D), BF16),
             dma((6,)), dma((2,)), dma((2,)),
-            dma((2, 7)), dma((2, 4, 3)), dma((2, 4)), dma((16,)),
-            dma((7,)), dma((4, 3)), dma((4,)), dma((4,)), dma((4, 4)), dma((4,)),
+            dma((2, 4)), dma((2, 4, 2)), dma((2, 4, 3)), dma((2, 4)), dma((16,)),
+            dma((2, 4)), dma((4, 3)), dma((4,)), dma((4,)), dma((4, 4)), dma((4,)),
             dma((3,)), dma((3,)), dma((4,)), dma((4,)), dma((4,)), dma((4,)),
             dma((2, 2, 4, 2)), dma((2, 2, 4, 2)), dma((2, 2, 4)), dma((2, 2, 4)),
             dma((2, 8)), dma((8,)), dma((2, 8)), dma((1,)), dma((1,)), dma((1,)), dma((1,)),

time: 155 us -> 124 us (0.80)
  the two profiles are of different devices: /device:TPU:21 before, /device:TPU:73 now
where the time goes in v3:
time: 124 us
  Pallas kernels  123 us (99%)
  local copies, waits for them, and re-layouts  1.7 us (1%)
    pallas_call x1, Pallas kernels, on_device(): pl.pallas_call(kernel, out_shape=jax.ShapeDtypeStruct((2, 64, D), BF16),...  123 us

profile of v3, /device:TPU:73, one launch (start us, length us, event | category | flops | bytes accessed | tf_op | source)
XLA Modules:
  0.0 124.3 jit_solution(12741518812827751808)
XLA Ops:
  0.0 122.6 %shard_map.64 = bf16[2,64,1152]{2,1,0:T(8,128)(2,1)} custom-call(bf16[2,64,1152]{2,1,0:T(8,128)(2,1)} %bitcast.12, f32[3,2,1152]{2,1,0:T(2,128)} %bitcast.17, bf16[18,1152]{1,0:T(8,128)(2,1)} %bitcast.15, bf16[36,1152]{1,0:T(8,128)(2,1)} %bitcast.13, bf16[18,1152]{1,0:T(8,128)(2,1)} %bitcast.16, bf16[36,1152]{1,0:T(8,128)(2,1)} %bitcast.14), custom_call_target="tpu_custom_call" | custom-call | tf_op jit(solution)/shard_map/pallas_call | solution.py:582
  122.6 1.7 %copy.8 = bf16[1,2,8,8,1152]{4,3,2,1,0:T(8,128)(2,1)} copy(bf16[1,2,8,8,1152]{4,3,2,1,0:T(8,128)(2,1)} %bitcast.11) | data formatting | bytes 589824

commit v4 on v3

--- a/solution.py
+++ b/solution.py
@@ -37,7 +37,7 @@
     lat_h, mod_h, wq_h, wkv_h, wo_h, wz_h, out,
     lat, mod, wq, wkv, wo, wz,
     wb, g1, g0, gb, kvo, kvl, kvr, ob, ab, ab0, bias, hid, rlat, rres, stage, res_s, q_s, wq_s,
-    in_s, lat_s, lat_r, w1y_s, w1t_s, w1x_s, w1s_s, w1_r, g1y_s, g1x_s, g1s_s, g1y_r, g1x_r, g1s_r,
+    in_s, lat_s, lat_r, w1y_s, w1t_s, w1x_s, w1s_s, w1_r, g1y_s, g1x_s, g1s_s, g1y_r, g1x_r, g1s_r, g1o_s, g1o_r,
     g0y_s, g0x_s, g0s_s, g0y_r, g0x_r, g0s_r, z_s, z_r, h_s, h_r, a_s, a_r, a0_r, o_s, o_r, r_s, r_r,
 ):
     b = lax.axis_index("branch")
@@ -282,6 +282,7 @@
     def g1_line(yk):
         for n in range(3):
             send(g1.at[c, x, yk], g1.at[c, x, yk], g1x_s.at[yk, n], g1x_r.at[x, yk], line[n])
+        send(g1.at[c, x, yk], g1.at[c, x, yk], g1o_s.at[yk], g1o_r.at[yk], sibling)
 
     def g1_send(s, way):
         at = (yy + 9 - s if way == 0 else yy + s - 1) % 8
@@ -316,7 +317,6 @@
                     sent(g1.at[c, x, at % 4], g1y_s.at[way, s - 1])
 
     def g1_core():
-        send(g1.at[c, x], g1.at[c, x], g1s_s.at[0], g1s_r.at[x], sibling)
         for k in range(1, 4):
             xk = (x + k) % 4
             for yk in range(4):
@@ -324,14 +324,17 @@
             send(g1.at[c, xk], g1.at[c, xk], g1s_s.at[k], g1s_r.at[xk], sibling)
 
     def g1_end():
-        for xk in range(4):
-            arrived(g1.at[1 - c, xk], g1s_r.at[xk])
+        for yk in range(4):
+            arrived(g1.at[1 - c, x, yk], g1o_r.at[yk])
+        for k in range(1, 4):
+            arrived(g1.at[1 - c, (x + k) % 4], g1s_r.at[(x + k) % 4])
 
     def g1_sent():
         for yk in range(4):
             for k in range(3):
                 sent(g1.at[c, x, yk], g1x_s.at[yk, k])
-        for k in range(4):
+            sent(g1.at[c, x, yk], g1o_s.at[yk])
+        for k in range(1, 4):
             sent(g1.at[c, (x + k) % 4], g1s_s.at[k])
 
     def g0_line():
@@ -479,27 +482,30 @@
 
     ring_step(1, 2)
     w1_line(1)
+    ring_step(1, 3)
     g1_take(1, 0)
     g1_take(1, 1)
-    ring_step(1, 3)
+    ring_step(1, 4)
     g1_take(2, 0)
     g1_take(2, 1)
-    ring_step(1, 4)
+    w1_core(1)
     ring_end(1)
-    w1_core(1)
+    w1_y(0, True)
     w1_end(1)
     pack_query(1)
-    for s in range(1, 5):
-        project(1, s)
+    project(1, 1)
+    project(1, 2)
     g1_take(3, 0)
     g1_take(3, 1)
-    w1_y(0, True)
+    project(1, 3)
+    project(1, 4)
+    g1_take(4, 0)
     halo_end(1)
+    w1_tree(0, True)
+    g0_y(True)
     attend(1)
-    g1_take(4, 0)
-    w1_tree(0, True)
+    w1_line(0)
     g1_core()
-    g0_y(True)
     attended()
     g1_end()
     control = (hid[...] + mod[2, 1:2, :] * out_project(1)).astype(BF16)
@@ -519,7 +525,12 @@
     gb[0, pl.ds(pl.multiple_of(64 * z, 64), 64), :] = normed(base_in, 0)
     ring_start(0, 0)
     ring_start(0, 1)
-    w1_line(0)
+    w1_core(0)
+
+    @pl.when(b == 0)
+    def _():
+        g0_line()
+
 
     @pl.when(b == 1)
     def _():
@@ -527,7 +538,6 @@
         send(res_s, rres, r_s.at[0], r_r.at[0], partner)
 
     ring_step(0, 2)
-    w1_core(0)
     w1_end(0)
     pack_query(0)
     project(0, 1)
@@ -540,14 +550,13 @@
 
     @pl.when(b == 0)
     def _():
-        g0_line()
+        g0_core()
 
     halo_end(0)
     attend(0)
 
     @pl.when(b == 0)
     def _():
-        g0_core()
         arrived(rres, r_r.at[0])
         attended_base()
         g0_end()
@@ -611,7 +620,7 @@
             vmem((HP, D), BF16),
             dma((6,)), dma((2,)), dma((2,)),
             dma((2, 4)), dma((2, 4, 2)), dma((2, 4, 3)), dma((2, 4)), dma((16,)),
-            dma((2, 4)), dma((4, 3)), dma((4,)), dma((4,)), dma((4, 4)), dma((4,)),
+            dma((2, 4)), dma((4, 3)), dma((4,)), dma((4,)), dma((4, 4)), dma((4,)), dma((4,)), dma((4,)),
             dma((3,)), dma((3,)), dma((4,)), dma((4,)), dma((4,)), dma((4,)),
             dma((2, 2, 4, 2)), dma((2, 2, 4, 2)), dma((2, 2, 4)), dma((2, 2, 4)),
             dma((2, 8)), dma((8,)), dma((2, 8)), dma((1,)), dma((1,)), dma((1,)), dma((1,)),

time: 124 us -> 111 us (0.90)
  the two profiles are of different devices: /device:TPU:73 before, /device:TPU:27 now
where the time goes in v4:
time: 111 us; the launch traced here: 110 us
  Pallas kernels  109 us (98%)
  local copies, waits for them, and re-layouts  1.7 us (2%)
    pallas_call x1, Pallas kernels, on_device(): pl.pallas_call(kernel, out_shape=jax.ShapeDtypeStruct((2, 64, D), BF16),...  109 us

profile of v4, /device:TPU:27, one launch (start us, length us, event | category | flops | bytes accessed | tf_op | source)
XLA Modules:
  0.0 110.4 jit_solution(7924732053256144997)
XLA Ops:
  0.0 108.7 %shard_map.64 = bf16[2,64,1152]{2,1,0:T(8,128)(2,1)} custom-call(bf16[2,64,1152]{2,1,0:T(8,128)(2,1)} %bitcast.12, f32[3,2,1152]{2,1,0:T(2,128)} %bitcast.17, bf16[18,1152]{1,0:T(8,128)(2,1)} %bitcast.15, bf16[36,1152]{1,0:T(8,128)(2,1)} %bitcast.13, bf16[18,1152]{1,0:T(8,128)(2,1)} %bitcast.16, bf16[36,1152]{1,0:T(8,128)(2,1)} %bitcast.14), custom_call_target="tpu_custom_call" | custom-call | tf_op jit(solution)/shard_map/pallas_call | solution.py:591
  108.7 1.7 %copy.8 = bf16[1,2,8,8,1152]{4,3,2,1,0:T(8,128)(2,1)} copy(bf16[1,2,8,8,1152]{4,3,2,1,0:T(8,128)(2,1)} %bitcast.11) | data formatting | bytes 589824

commit v5 on v4

--- a/solution.py
+++ b/solution.py
@@ -36,7 +36,7 @@
 def kernel(
     lat_h, mod_h, wq_h, wkv_h, wo_h, wz_h, out,
     lat, mod, wq, wkv, wo, wz,
-    wb, g1, g0, gb, kvo, kvl, kvr, ob, ab, ab0, bias, hid, rlat, rres, stage, res_s, q_s, wq_s,
+    wb, g1, g0, gb, kvo, kvl, kvr, ob, ab, ab0, bias, hid, rlat, rres, stage, res_s, q_s, wq_s, wo_s,
     in_s, lat_s, lat_r, w1y_s, w1t_s, w1x_s, w1s_s, w1_r, g1y_s, g1x_s, g1s_s, g1y_r, g1x_r, g1s_r, g1o_s, g1o_r,
     g0y_s, g0x_s, g0s_s, g0y_r, g0x_r, g0s_r, z_s, z_r, h_s, h_r, a_s, a_r, a0_r, o_s, o_r, r_s, r_r,
 ):
@@ -75,8 +75,8 @@
         ).wait_send()
 
     barrier = pltpu.get_barrier_semaphore()
-    across = [(1 - b, (z + k) % 8, t) for k in range(1, 8)]
-    peers = column + line + ring + across + [sibling, (b, z, far)]
+    near = [column[k - 1] for k in (1, 2, 4, 6, 7)]
+    peers = near + line + [ring[0], ring[6], sibling, (b, z, far)]
     for dev in peers:
         pl.semaphore_signal(barrier, inc=1, device_id=dev, device_id_type=MESH)
 
@@ -435,8 +435,7 @@
             def _():
                 sent(ob.at[copy, pl.ds(64 * tile, 64)], a_s.at[copy, tile])
 
-    def out_project(copy):
-        total = None
+    def pack_out(copy):
         for head in range(8):
             parts = []
             for n in range(4):
@@ -445,12 +444,16 @@
                     parts.append(g1[at].astype(F32)[40:64])
                 else:
                     parts.append(g0[at].astype(F32)[0:GP])
-            w_head = jnp.concatenate(parts, axis=0).astype(BF16)
+            wo_s[HP * head : HP * head + HP, :] = jnp.concatenate(parts, axis=0).astype(BF16)
+
+    def out_project(copy):
+        total = None
+        for head in range(8):
             if copy == 1:
                 mixed = ab[head][:, 0:HP]
             else:
                 mixed = jnp.concatenate([ab0[0, head][:, 0:HP], ab0[1, head][:, 0:HP]], axis=0)
-            part = dot(mixed, w_head, NN)
+            part = dot(mixed, wo_s[HP * head : HP * head + HP, :], NN)
             total = part if total is None else total + part
         return total
 
@@ -506,8 +509,9 @@
     attend(1)
     w1_line(0)
     g1_core()
+    g1_end()
+    pack_out(1)
     attended()
-    g1_end()
     control = (hid[...] + mod[2, 1:2, :] * out_project(1)).astype(BF16)
 
     @pl.when(b == 0)
@@ -557,9 +561,10 @@
 
     @pl.when(b == 0)
     def _():
+        g0_end()
+        pack_out(0)
         arrived(rres, r_r.at[0])
         attended_base()
-        g0_end()
         second = lat[1].astype(F32) + rres[...].astype(F32)
         gated = mod[2, 0:1, :] * out_project(0)
         out[0] = (hid[...] + gated[0:64]).astype(BF16)
@@ -618,6 +623,7 @@
             vmem((64, D), BF16),
             vmem((512, HP), BF16),
             vmem((HP, D), BF16),
+            vmem((8 * HP, D), BF16),
             dma((6,)), dma((2,)), dma((2,)),
             dma((2, 4)), dma((2, 4, 2)), dma((2, 4, 3)), dma((2, 4)), dma((16,)),
             dma((2, 4)), dma((4, 3)), dma((4,)), dma((4,)), dma((4, 4)), dma((4,)), dma((4,)), dma((4,)),

time: 111 us -> 109 us (0.982)
  Pallas kernels: 109 us -> 107 us
    pallas_call x1, Pallas kernels: 109 us -> 107 us  [on_device(): pl.pallas_call(kernel, out_shape=jax.ShapeDtypeStruct((2, 64, D), BF16),...]
where the time goes in v5:
time: 109 us
  Pallas kernels  107 us (98%)
  local copies, waits for them, and re-layouts  1.7 us (2%)
    pallas_call x1, Pallas kernels, on_device(): pl.pallas_call(kernel, out_shape=jax.ShapeDtypeStruct((2, 64, D), BF16),...  107 us

profile of v5, /device:TPU:27, one launch (start us, length us, event | category | flops | bytes accessed | tf_op | source)
XLA Modules:
  0.0 108.9 jit_solution(14166537987206410019)
XLA Ops:
  0.0 107.2 %shard_map.64 = bf16[2,64,1152]{2,1,0:T(8,128)(2,1)} custom-call(bf16[2,64,1152]{2,1,0:T(8,128)(2,1)} %bitcast.12, f32[3,2,1152]{2,1,0:T(2,128)} %bitcast.17, bf16[18,1152]{1,0:T(8,128)(2,1)} %bitcast.15, bf16[36,1152]{1,0:T(8,128)(2,1)} %bitcast.13, bf16[18,1152]{1,0:T(8,128)(2,1)} %bitcast.16, bf16[36,1152]{1,0:T(8,128)(2,1)} %bitcast.14), custom_call_target="tpu_custom_call" | custom-call | tf_op jit(solution)/shard_map/pallas_call | solution.py:596
  107.2 1.7 %copy.8 = bf16[1,2,8,8,1152]{4,3,2,1,0:T(8,128)(2,1)} copy(bf16[1,2,8,8,1152]{4,3,2,1,0:T(8,128)(2,1)} %bitcast.11) | data formatting | bytes 589824

commit v6 on v5

--- a/solution.py
+++ b/solution.py
@@ -36,7 +36,7 @@
 def kernel(
     lat_h, mod_h, wq_h, wkv_h, wo_h, wz_h, out,
     lat, mod, wq, wkv, wo, wz,
-    wb, g1, g0, gb, kvo, kvl, kvr, ob, ab, ab0, bias, hid, rlat, rres, stage, res_s, q_s, wq_s, wo_s,
+    wb, g1, g0, gb, kvo, kvl, kvr, ob, ab, ab0, bias, hid, rlat, rres, stage, res_s, q_s, wq_s, wo_s, wz_s,
     in_s, lat_s, lat_r, w1y_s, w1t_s, w1x_s, w1s_s, w1_r, g1y_s, g1x_s, g1s_s, g1y_r, g1x_r, g1s_r, g1o_s, g1o_r,
     g0y_s, g0x_s, g0s_s, g0y_r, g0x_r, g0s_r, z_s, z_r, h_s, h_r, a_s, a_r, a0_r, o_s, o_r, r_s, r_r,
 ):
@@ -447,23 +447,26 @@
             wo_s[HP * head : HP * head + HP, :] = jnp.concatenate(parts, axis=0).astype(BF16)
 
     def out_project(copy):
-        total = None
-        for head in range(8):
-            if copy == 1:
-                mixed = ab[head][:, 0:HP]
-            else:
-                mixed = jnp.concatenate([ab0[0, head][:, 0:HP], ab0[1, head][:, 0:HP]], axis=0)
-            part = dot(mixed, wo_s[HP * head : HP * head + HP, :], NN)
-            total = part if total is None else total + part
-        return total
-
-    def zero_project(control):
-        parts = []
+        if copy == 1:
+            mixed = jnp.concatenate([ab[head][:, 0:HP] for head in range(8)], axis=1)
+        else:
+            mixed = jnp.concatenate(
+                [
+                    jnp.concatenate([ab0[image, head][:, 0:HP] for head in range(8)], axis=1)
+                    for image in range(2)
+                ],
+                axis=0,
+            )
+        return dot(mixed, wo_s[...], NN)
+
+    def pack_zero():
         for pair in range(16):
             two = [g1[core, pair // 4, pair % 4].astype(F32)[0:40] for core in range(2)]
-            wide = dot(control, jnp.concatenate(two, axis=0).astype(BF16), NT)
-            parts += [wide[:, 0:36], wide[:, 40:76]]
-        return jnp.concatenate(parts, axis=1).astype(BF16)
+            wz_s[80 * pair : 80 * pair + 80, :] = jnp.concatenate(two, axis=0).astype(BF16)
+
+    def zero_project(control):
+        wide = dot(control, wz_s[...], NT)
+        return jnp.concatenate([wide[:, 40 * n : 40 * n + 36] for n in range(32)], axis=1).astype(BF16)
 
     for load in loads[4:]:
         load.wait()
@@ -511,6 +514,7 @@
     g1_core()
     g1_end()
     pack_out(1)
+    pack_zero()
     attended()
     control = (hid[...] + mod[2, 1:2, :] * out_project(1)).astype(BF16)
 
@@ -624,6 +628,7 @@
             vmem((512, HP), BF16),
             vmem((HP, D), BF16),
             vmem((8 * HP, D), BF16),
+            vmem((1280, D), BF16),
             dma((6,)), dma((2,)), dma((2,)),
             dma((2, 4)), dma((2, 4, 2)), dma((2, 4, 3)), dma((2, 4)), dma((16,)),
             dma((2, 4)), dma((4, 3)), dma((4,)), dma((4,)), dma((4, 4)), dma((4,)), dma((4,)), dma((4,)),

time: 109 us -> 109 us (level)
  no operation moved by 1% of the time
where the time goes in v6:
time: 109 us
  Pallas kernels  107 us (98%)
  local copies, waits for them, and re-layouts  1.7 us (2%)
    pallas_call x1, Pallas kernels, on_device(): pl.pallas_call(kernel, out_shape=jax.ShapeDtypeStruct((2, 64, D), BF16),...  107 us

profile of v6, /device:TPU:27, one launch (start us, length us, event | category | flops | bytes accessed | tf_op | source)
XLA Modules:
  0.0 108.6 jit_solution(1606046776966295544)
XLA Ops:
  0.0 106.9 %shard_map.64 = bf16[2,64,1152]{2,1,0:T(8,128)(2,1)} custom-call(bf16[2,64,1152]{2,1,0:T(8,128)(2,1)} %bitcast.12, f32[3,2,1152]{2,1,0:T(2,128)} %bitcast.17, bf16[18,1152]{1,0:T(8,128)(2,1)} %bitcast.15, bf16[36,1152]{1,0:T(8,128)(2,1)} %bitcast.13, bf16[18,1152]{1,0:T(8,128)(2,1)} %bitcast.16, bf16[36,1152]{1,0:T(8,128)(2,1)} %bitcast.14), custom_call_target="tpu_custom_call" | custom-call | tf_op jit(solution)/shard_map/pallas_call | solution.py:600
  106.9 1.7 %copy.8 = bf16[1,2,8,8,1152]{4,3,2,1,0:T(8,128)(2,1)} copy(bf16[1,2,8,8,1152]{4,3,2,1,0:T(8,128)(2,1)} %bitcast.11) | data formatting | bytes 589824

commit v7 on v6

--- a/solution.py
+++ b/solution.py
@@ -34,8 +34,8 @@
 
 
 def kernel(
-    lat_h, mod_h, wq_h, wkv_h, wo_h, wz_h, out,
-    lat, mod, wq, wkv, wo, wz,
+    lat_h, mod, wq, wkv, wo, wz, out,
+    lat,
     wb, g1, g0, gb, kvo, kvl, kvr, ob, ab, ab0, bias, hid, rlat, rres, stage, res_s, q_s, wq_s, wo_s, wz_s,
     in_s, lat_s, lat_r, w1y_s, w1t_s, w1x_s, w1s_s, w1_r, g1y_s, g1x_s, g1s_s, g1y_r, g1x_r, g1s_r, g1o_s, g1o_r,
     g0y_s, g0x_s, g0s_s, g0y_r, g0x_r, g0s_r, z_s, z_r, h_s, h_r, a_s, a_r, a0_r, o_s, o_r, r_s, r_r,
@@ -80,16 +80,8 @@
     for dev in peers:
         pl.semaphore_signal(barrier, inc=1, device_id=dev, device_id_type=MESH)
 
-    loads = [
-        pltpu.make_async_copy(src, dst, in_s.at[n])
-        for n, (src, dst) in enumerate(
-            ((wq_h, wq), (wkv_h, wkv), (wo_h, wo), (wz_h, wz), (lat_h, lat), (mod_h, mod))
-        )
-    ]
-    for load in loads:
-        load.start()
-    for load in loads[:4]:
-        load.wait()
+    load = pltpu.make_async_copy(lat_h, lat, in_s.at[0])
+    load.start()
 
     rows = (
         dot(pick(144, 18, [(0, 0, 18)]), wq[...], NN)
@@ -468,8 +460,7 @@
         wide = dot(control, wz_s[...], NT)
         return jnp.concatenate([wide[:, 40 * n : 40 * n + 36] for n in range(32)], axis=1).astype(BF16)
 
-    for load in loads[4:]:
-        load.wait()
+    load.wait()
     for h in range(2):
         part = pl.ds(32 * h, 32)
         arrived(rlat.at[part], lat_r.at[h])
@@ -600,15 +591,10 @@
     result = pl.pallas_call(
         kernel,
         out_shape=jax.ShapeDtypeStruct((2, 64, D), BF16),
-        in_specs=[pl.BlockSpec(memory_space=pl.ANY)] * 6,
+        in_specs=[pl.BlockSpec(memory_space=pl.ANY)] + [pl.BlockSpec(memory_space=pltpu.VMEM)] * 5,
         out_specs=pl.BlockSpec(memory_space=pltpu.VMEM),
         scratch_shapes=[
             vmem((2, 64, D), BF16),
-            vmem((3, 2, D), F32),
-            vmem((18, D), BF16),
-            vmem((36, D), BF16),
-            vmem((18, D), BF16),
-            vmem((36, D), BF16),
             vmem((2, 320, D), BF16),
             vmem((2, 4, 4, 64, D), BF16),
             vmem((2, 4, 4, 32, D), BF16),
@@ -629,7 +615,7 @@
             vmem((HP, D), BF16),
             vmem((8 * HP, D), BF16),
             vmem((1280, D), BF16),
-            dma((6,)), dma((2,)), dma((2,)),
+            dma((1,)), dma((2,)), dma((2,)),
             dma((2, 4)), dma((2, 4, 2)), dma((2, 4, 3)), dma((2, 4)), dma((16,)),
             dma((2, 4)), dma((4, 3)), dma((4,)), dma((4,)), dma((4, 4)), dma((4,)), dma((4,)), dma((4,)),
             dma((3,)), dma((3,)), dma((4,)), dma((4,)), dma((4,)), dma((4,)),

time: 109 us -> 110 us (level)
  no operation moved by 1% of the time
where the time goes in v7:
time: 110 us; the launch traced here: 109 us
  Pallas kernels  108 us (98%)
  local copies, waits for them, and re-layouts  1.7 us (2%)
    pallas_call x1, Pallas kernels, on_device(): pl.pallas_call(kernel, out_shape=jax.ShapeDtypeStruct((2, 64, D), BF16),...  108 us

profile of v7, /device:TPU:27, one launch (start us, length us, event | category | flops | bytes accessed | tf_op | source)
XLA Modules:
  0.0 109.3 jit_solution(8793181266790747773)
XLA Ops:
  0.0 107.6 %shard_map.64 = bf16[2,64,1152]{2,1,0:T(8,128)(2,1)} custom-call(bf16[2,64,1152]{2,1,0:T(8,128)(2,1)} %bitcast.12, f32[3,2,1152]{2,1,0:T(2,128)} %bitcast.17, bf16[18,1152]{1,0:T(8,128)(2,1)} %bitcast.15, bf16[36,1152]{1,0:T(8,128)(2,1)} %bitcast.13, bf16[18,1152]{1,0:T(8,128)(2,1)} %bitcast.16, bf16[36,1152]{1,0:T(8,128)(2,1)} %bitcast.14), custom_call_target="tpu_custom_call" | custom-call | tf_op jit(solution)/shard_map/pallas_call | solution.py:591
  107.6 1.7 %copy.8 = bf16[1,2,8,8,1152]{4,3,2,1,0:T(8,128)(2,1)} copy(bf16[1,2,8,8,1152]{4,3,2,1,0:T(8,128)(2,1)} %bitcast.11) | data formatting | bytes 589824

commit v8 on v7

--- a/solution.py
+++ b/solution.py
@@ -501,8 +501,8 @@
     w1_tree(0, True)
     g0_y(True)
     attend(1)
+    g1_core()
     w1_line(0)
-    g1_core()
     g1_end()
     pack_out(1)
     pack_zero()

time: 110 us -> 109 us (level)
  the two profiles are of different devices: /device:TPU:27 before, /device:TPU:21 now
where the time goes in v8:
time: 109 us
  Pallas kernels  107 us (98%)
  local copies, waits for them, and re-layouts  1.7 us (2%)
    pallas_call x1, Pallas kernels, on_device(): pl.pallas_call(kernel, out_shape=jax.ShapeDtypeStruct((2, 64, D), BF16),...  107 us

profile of v8, /device:TPU:21, one launch (start us, length us, event | category | flops | bytes accessed | tf_op | source)
XLA Modules:
  0.0 108.9 jit_solution(17633009537030830931)
XLA Ops:
  0.0 107.2 %shard_map.64 = bf16[2,64,1152]{2,1,0:T(8,128)(2,1)} custom-call(bf16[2,64,1152]{2,1,0:T(8,128)(2,1)} %bitcast.12, f32[3,2,1152]{2,1,0:T(2,128)} %bitcast.17, bf16[18,1152]{1,0:T(8,128)(2,1)} %bitcast.15, bf16[36,1152]{1,0:T(8,128)(2,1)} %bitcast.13, bf16[18,1152]{1,0:T(8,128)(2,1)} %bitcast.16, bf16[36,1152]{1,0:T(8,128)(2,1)} %bitcast.14), custom_call_target="tpu_custom_call" | custom-call | tf_op jit(solution)/shard_map/pallas_call | solution.py:591
  107.2 1.7 %copy.8 = bf16[1,2,8,8,1152]{4,3,2,1,0:T(8,128)(2,1)} copy(bf16[1,2,8,8,1152]{4,3,2,1,0:T(8,128)(2,1)} %bitcast.11) | data formatting | bytes 589824
